TPU v7x, 32 devices: a whole 2x2x4 slice. The times are simulated.
32 devices in a mesh: ta: 4 (over y, x), sa: 8 (over z, core).
Axes of the slice: x: 2, y: 2, z: 4, core: 2. Of those that a mesh axis runs over, the one named last changes fastest.
Arguments:
- snapshots: float32 [256, 2, 32768], P('ta', None, 'sa'), may hold values from -6 to 6
- bins: int32 [16], replicated, may hold values from 0 to 127, as said below
- eigenvalues: float32 [16, 32], P('ta'), may hold values from 100 to 1000
- old_basis: bfloat16 [16, 2, 32, 2, 32768], P('ta', None, None, None, 'sa'), may hold values from -0.015625 to 0.015625, as said below
- block_count: int32 [1], replicated, may hold values from 1 to 8
Outputs:
- new_basis: bfloat16 [16, 2, 32, 2, 32768], P('ta', None, None, None, 'sa')
- coherence: float32 [16, 2, 32, 32], P('ta')
Inputs may be any that keep to these rules, and one draw needn't show every extreme that they name: The 16 bins are distinct; 0 and 127 are always among them. `old_basis`: every entry lies within 4 / sqrt(65536) in magnitude.
All inputs are finite; a program needn't handle non-finite values.
Results may differ from a plain program's by a relative error of at most 0.001.
Values sent between devices are 32-bit elements; how exact they have to be, the bound alone decides.
A program may use at most 128 MiB of HBM per device.

v0:
```python
import math

import jax
import jax.numpy as jnp
from jax import lax
from jax.sharding import PartitionSpec as P


def tables(bins, times, total):
    phase = bins[:, None] * times[None, :] % total
    angle = 2.0 * math.pi / total * phase.astype(jnp.float32)
    window = 0.5 - 0.5 * jnp.cos(2.0 * math.pi / total * times.astype(jnp.float32))
    scale = math.sqrt(8.0 / (3.0 * total))
    return (jnp.cos(angle) * window[None, :] * scale, -jnp.sin(angle) * window[None, :] * scale)


def pair_dot(left, right, form):
    return jnp.einsum(form, left, right, precision=lax.Precision.HIGHEST)


def local(snapshots, bins, eigenvalues, old_basis, block_count):
    hi = lax.Precision.HIGHEST
    slice_len = snapshots.shape[0]
    points = snapshots.shape[2]
    groups = lax.axis_size("ta")
    total = slice_len * groups
    times = lax.axis_index("ta") * slice_len + jnp.arange(slice_len, dtype=jnp.int32)
    c_tab, s_tab = tables(bins, times, total)
    flat = snapshots.reshape(slice_len, 2 * points)
    terms = jnp.stack(
        [jnp.dot(c_tab, flat, precision=hi), jnp.dot(s_tab, flat, precision=hi)], axis=1
    )
    spec = lax.psum_scatter(terms, "ta", scatter_dimension=0, tiled=True)
    local_bins = spec.shape[0]
    rank = old_basis.shape[2]
    basis = old_basis.reshape(local_bins, 2, rank, 2 * points).astype(jnp.float32)
    u_re = basis[:, 0]
    u_im = basis[:, 1]
    s_re = spec[:, 0]
    s_im = spec[:, 1]
    c_re = pair_dot(u_re, s_re, "bjm,bm->bj") + pair_dot(u_im, s_im, "bjm,bm->bj")
    c_im = pair_dot(u_re, s_im, "bjm,bm->bj") - pair_dot(u_im, s_re, "bjm,bm->bj")
    count = block_count[0].astype(jnp.float32)
    w_old = count / (count + 1.0)
    w_new = 1.0 / (count + 1.0)
    scaled = w_old * eigenvalues
    c_re, c_im = lax.psum((c_re, c_im), "sa")
    g_re = scaled[:, :, None] * u_re + w_new * (
        c_re[:, :, None] * s_re[:, None, :] + c_im[:, :, None] * s_im[:, None, :]
    )
    g_im = scaled[:, :, None] * u_im + w_new * (
        c_re[:, :, None] * s_im[:, None, :] - c_im[:, :, None] * s_re[:, None, :]
    )
    part_re = pair_dot(g_re, g_re, "bjm,bkm->bjk") + pair_dot(g_im, g_im, "bjm,bkm->bjk")
    part_im = pair_dot(g_re, g_im, "bjm,bkm->bjk") - pair_dot(g_im, g_re, "bjm,bkm->bjk")
    gram_re, gram_im = lax.psum((part_re, part_im), "sa")
    inv = 1.0 / jnp.sqrt(jnp.diagonal(gram_re, axis1=1, axis2=2) + 1e-06)
    fresh = jnp.stack([g_re * inv[:, :, None], g_im * inv[:, :, None]], axis=1).astype(jnp.bfloat16)
    outer = inv[:, :, None] * inv[:, None, :]
    coherence = jnp.stack([gram_re * outer, gram_im * outer], axis=1)
    return (fresh.reshape(old_basis.shape), coherence)


def solution(mesh):
    return jax.shard_map(
        local,
        mesh=mesh,
        in_specs=(P("ta", None, "sa"), P(), P("ta", None), P("ta", None, None, None, "sa"), P()),
        out_specs=(P("ta", None, None, None, "sa"), P("ta", None, None, None)),
        check_vma=False,
    )
```

profile of v0, /device:TPU:0, one launch (start us, length us, event | category | flops | bytes accessed | tf_op | source)
XLA Modules:
  0.0 197.5 jit_solution(18443441524452468215)
XLA Ops:
  7.2 0.0 copy-start.2
  7.2 0.0 all-reduce.5.cloned.1.call-start
  7.3 2.8 %copy.27 = f32[8,8,2,4096]{3,1,2,0:T(8,128)S(1)} copy(f32[8,8,2,4096]{3,2,1,0:T(2,128)} %bitcast.68) | data formatting | bytes 4194304
  10.1 0.0 copy-done.2
  10.1 1.2 convolution_bitcast_fusion
  11.3 1.2 convolution_bitcast_fusion.1
  12.5 1.0 pad_maximum_fusion.1
  13.5 0.0 all-reduce.5.cloned.1.call-update
  13.5 7.8 %reshape.63 = bf16[4,2,32,8192]{3,2,1,0:T(8,128)(2,1)} reshape(bf16[4,2,32,2,4096]{4,3,2,1,0:T(2,128)(2,1)} %param.8) | data formatting | bytes 8388608 | tf_op jit(solution)/shard_map/reshape | solution.py:36
  21.3 0.0 copy-start.3
  21.3 0.0 copy-start.1
  21.3 6.5 %copy_convert_fusion = f32[4,2,32,8192]{3,2,0,1:T(8,128)} fusion(bf16[4,2,32,8192]{3,2,1,0:T(8,128)(2,1)} %reshape.63), kind=kLoop, calls=%fused_computation.8 | loop fusion | flops 2097152 | bytes 12582912 | tf_op jit(solution)/shard_map/convert_element_type | solution.py:36
  28.6 0.0 copy-done.3
  28.6 0.6 dynamic-slice
  29.8 0.0 copy-done.1
  29.9 39.1 %all-reduce.5.cloned.1.call-done = f32[16,2,8192]{2,0,1:T(8,128)} async-done(((f32[16,2,8192]{2,0,1:T(8,128)}), f32[16,2,8192]{2,0,1:T(8,128)}) %all-reduce.5.cloned.1.call-update) | async-done | bytes 1048592
  68.9 0.0 copy-start
  68.9 1.3 dynamic-slice_bitcast_fusion.1
  70.2 3.5 %fusion.4 = f32[4,1,32]{2,1,0:T(1,128)S(1)} fusion(bf16[4,2,32,8192]{3,2,1,0:T(8,128)(2,1)} %reshape.63, f32[4,8192,1]{1,0,2:T(4,128)S(1)} %get-tuple-element.14), kind=kOutput, calls=%fused_computation.15 | convolution fusion | flops 12582912 | bytes 2228736 | tf_op jit(solution)/shard_map/bjm,bm->bj/dot_general | solution.py:18
  73.7 3.3 %fusion.3 = f32[4,1,32]{2,1,0:T(1,128)S(1)} fusion(bf16[4,2,32,8192]{3,2,1,0:T(8,128)(2,1)} %reshape.63, f32[4,8192,1]{1,0,2:T(4,128)S(1)} %get-tuple-element.14), kind=kOutput, calls=%fused_computation.14 | convolution fusion | flops 12582912 | bytes 2228736 | tf_op jit(solution)/shard_map/bjm,bm->bj/dot_general | solution.py:18
  77.0 0.0 copy-done
  77.0 1.7 fusion.2
  78.7 1.7 fusion.5
  80.5 16.6 %all-reduce.2 = (f32[4,32]{1,0:T(4,128)S(1)}, f32[4,32]{1,0:T(4,128)S(1)}) all-reduce(f32[4,32]{1,0:T(4,128)S(1)} %sub.26, f32[4,32]{1,0:T(4,128)S(1)} %add.85), channel_id=1, replica_groups=mesh['ta'=4,'sa'=8] {'sa'}, use_global_device_ids=true, to_apply=%region_2.3 | all-reduce | flops 256 | bytes 2048 | tf_op jit(solution)/shard_map/psum | solution.py:47
  97.1 0.0 slice-start
  97.1 9.2 %fusion.9 = f32[4,32,32]{2,1,0:T(8,128)S(1)} fusion(f32[4,2,32,8192]{3,2,0,1:T(8,128)} %copy_convert_fusion, f32[4,8192]{1,0:T(4,128)S(1)} %get-tuple-element.15, f32[4,32]{1,0:T(4,128)S(1)} %get-tuple-element.8, f32[4,8192]{1,0:T(4,128)S(1)} %get-tuple-element.12, f32[4,32]{1,0:T(4,128)S(1)} %get-tuple-element.9, f32[]{:T(128)S(6)} %div.9, ...), kind=kOutput, calls=%fused_computation.21 | convolution fusion | flops 408944640 | bytes 4474372 | tf_op jit(solution)/shard_map/bjm,bkm->bjk/dot_general | solution.py:18
  106.3 0.0 slice-start.1
  106.3 9.2 %fusion.7 = f32[4,32,32]{2,1,0:T(8,128)S(1)} fusion(f32[4,2,32,8192]{3,2,0,1:T(8,128)} %copy_convert_fusion, f32[4,8192]{1,0:T(4,128)S(1)} %get-tuple-element.15, f32[4,32]{1,0:T(4,128)S(1)} %get-tuple-element.8, f32[4,8192]{1,0:T(4,128)S(1)} %get-tuple-element.12, f32[4,32]{1,0:T(4,128)S(1)} %get-tuple-element.9, f32[]{:T(128)S(6)} %div.9, ...), kind=kOutput, calls=%fused_computation.20 | convolution fusion | flops 415236096 | bytes 8942592 | tf_op jit(solution)/shard_map/bjm,bkm->bjk/dot_general | solution.py:18
  115.6 0.0 slice-done
  115.6 0.0 slice-done.1
  115.6 16.7 %convolution_add_fusion = f32[4,32,32]{2,1,0:T(8,128)S(1)} fusion(f32[4,32,32]{2,1,0:T(8,128)S(1)} %fusion.9, f32[4,2,32,8192]{3,2,0,1:T(8,128)S(1)} %bitcast.65, f32[4,8192]{1,0:T(4,128)S(1)} %get-tuple-element.15, f32[4,32]{1,0:T(4,128)S(1)} %get-tuple-element.8, f32[4,8192]{1,0:T(4,128)S(1)} %get-tuple-element.12, f32[4,32]{1,0:T(4,128)S(1)} %get-tuple-element.9, ...), kind=kOutput, calls=%fused_computation.18 | convolution fusion | flops 408948736 | bytes 4544516 | tf_op jit(solution)/shard_map/bjm,bkm->bjk/dot_general | solution.py:18
  132.4 6.0 %convolution_subtract_fusion = f32[4,32,32]{2,1,0:T(8,128)S(1)} fusion(f32[4,32,32]{2,1,0:T(8,128)S(1)} %fusion.7, f32[4,2,32,8192]{3,2,0,1:T(8,128)S(1)} %bitcast.65, f32[4,8192]{1,0:T(4,128)S(1)} %get-tuple-element.15, f32[4,32]{1,0:T(4,128)S(1)} %get-tuple-element.8, f32[4,8192]{1,0:T(4,128)S(1)} %get-tuple-element.12, ...), kind=kOutput, calls=%fused_computation.17 | convolution fusion | flops 415240192 | bytes 9008128 | tf_op jit(solution)/shard_map/bjm,bkm->bjk/dot_general | solution.py:18
  138.3 27.2 %all-reduce.1 = (f32[4,32,32]{2,1,0:T(8,128)S(1)}, f32[4,32,32]{2,1,0:T(8,128)S(1)}) all-reduce(f32[4,32,32]{2,1,0:T(8,128)S(1)} %convolution_add_fusion, f32[4,32,32]{2,1,0:T(8,128)S(1)} %convolution_subtract_fusion), channel_id=1, replica_groups=mesh['ta'=4,'sa'=8] {'sa'}, use_global_device_ids=true, to_apply=%region_3.4 | all-reduce | flops 8192 | bytes 65536 | tf_op jit(solution)/shard_map/psum | solution.py:56
  165.5 0.3 copy.14
  165.8 0.7 gather_fusion
  166.5 0.1 copy.15
  166.6 5.5 %multiply_convert_fusion.1 = (bf16[4,1,32,8192]{3,2,0,1:T(8,128)(2,1)}, bf16[4,1,32,8192]{3,2,0,1:T(8,128)(2,1)S(1)}) fusion(f32[4,2,32,8192]{3,2,0,1:T(8,128)} %copy_convert_fusion, f32[4,32]{1,0:T(4,128)S(1)} %copy.15, f32[4,8192]{1,0:T(4,128)S(1)} %get-tuple-element.15, f32[4,32]{1,0:T(4,128)S(1)} %get-tuple-element.8, ...), kind=kLoop, calls=%fused_computation.10 | loop fusion | flops 16777216 | bytes 12847108 | tf_op jit(solution)/shard_map/convert.3
  172.1 0.1 fusion.18
  172.3 0.7 copy.18
  172.9 4.5 %stack.30 = bf16[4,1,32,2,4096]{4,3,2,1,0:T(2,128)(2,1)} reshape(bf16[4,1,32,8192]{3,2,0,1:T(8,128)(2,1)} %get-tuple-element.10) | data formatting | bytes 4194304 | tf_op jit(solution)/shard_map/stack | solution.py:58
  177.4 2.7 %stack.31 = bf16[4,1,32,2,4096]{4,3,2,1,0:T(2,128)(2,1)} reshape(bf16[4,1,32,8192]{3,2,0,1:T(8,128)(2,1)S(1)} %get-tuple-element.11) | data formatting | bytes 4194304 | tf_op jit(solution)/shard_map/stack | solution.py:58
  180.1 10.4 %pad_maximum_fusion = bf16[4,2,32,2,4096]{4,3,2,1,0:T(2,128)(2,1)} fusion(bf16[4,1,32,2,4096]{4,3,2,1,0:T(2,128)(2,1)} %stack.31, bf16[4,1,32,2,4096]{4,3,2,1,0:T(2,128)(2,1)} %stack.30), kind=kLoop, calls=%fused_computation.3 | loop fusion | flops 2097152 | bytes 8388608 | tf_op jit(solution)/shard_map/stack | solution.py:58
  (9 shorter events, 0.1 us)
Async XLA Ops:
  7.2 2.9 %copy-start.2 = (s32[16]{0:T(128)S(1)}, s32[16]{0:T(128)}, u32[]{:S(2)}) copy-start(s32[16]{0:T(128)} %param.6) | copy-start | bytes 196
  7.2 61.8 %all-reduce.5.cloned.1.call-start = ((), (), s32[]{:S(2)}) async-start(), calls=%async_computation | async-start | bytes 2097152
  21.3 7.3 %copy-start.3 = (u32[32]{0:T(128)S(1)}, u32[32]{0:T(128)}, u32[]{:S(2)}) copy-start(u32[32]{0:T(128)} %constant.54) | copy-start | bytes 388
  21.3 8.5 %copy-start.1 = (f32[4,32]{1,0:T(4,128)S(1)}, f32[4,32]{1,0:T(4,128)}, u32[]{:S(2)}) copy-start(f32[4,32]{1,0:T(4,128)} %param.7) | copy-start | bytes 1540
  68.9 8.1 %copy-start = (bf16[4,2,32,8192]{3,2,1,0:T(8,128)(2,1)S(1)}, bf16[4,2,32,8192]{3,2,1,0:T(8,128)(2,1)}, u32[]{:S(2)}) copy-start(bf16[4,2,32,8192]{3,2,1,0:T(8,128)(2,1)} %reshape.63) | copy-start | bytes 12582916
  97.1 18.5 %slice-start = ((s8[8388608]{0:T(1024)(128)(4,1)}), s8[4194304]{0:T(1024)(128)(4,1)S(1)}, s32[]{:S(2)}) async-start(s8[8388608]{0:T(1024)(128)(4,1)} %bitcast.64), calls=%async_computation.1 | async-start | bytes 8388608
  106.3 9.3 %slice-start.1 = ((s8[8388608]{0:T(1024)(128)(4,1)}), s8[4194304]{0:T(1024)(128)(4,1)S(1)}, s32[]{:S(2)}) async-start(s8[8388608]{0:T(1024)(128)(4,1)} %bitcast.64), calls=%async_computation.2 | async-start | bytes 8388608
Sparse Core Ops, SparseCore 0:
  13.6 55.2 all-reduce.4
where the time goes:
time: 200 us; the launch traced here: 198 us
  matrix products  53.8 us (27%)
  blocking collectives  43.8 us (22%)
  waiting for transfers between devices  39.1 us (20%)
  other arithmetic  23.6 us (12%)
  local copies, waits for them, and re-layouts  21.4 us (11%)
  between operations  15.8 us (8%)
    dot_general x8, matrix products, pair_dot(): return jnp.einsum(form, left, right, precision=lax.Precision.HIGHEST)  51.5 us
    unnamed x2, waiting for transfers between devices  39.1 us
    psum x1, blocking collectives, local(): gram_re, gram_im = lax.psum((part_re, part_im), 'sa')  27.2 us
    psum x1, blocking collectives, local(): c_re, c_im = lax.psum((c_re, c_im), 'sa')  16.6 us
    another operation x1, other arithmetic, local(): jnp.stack([g_re * inv[:, :, None], g_im * inv[:, :, None]], axis=1)  10.4 us
    reshape x1, local copies, waits for them, and re-layouts, local(): old_basis.reshape(local_bins, 2, rank, 2 * points).astype(jnp.float32)  7.8 us
    another operation x2, local copies, waits for them, and re-layouts, local(): jnp.stack([g_re * inv[:, :, None], g_im * inv[:, :, None]], axis=1)  7.2 us
    convert_element_type x1, other arithmetic, local(): old_basis.reshape(local_bins, 2, rank, 2 * points).astype(jnp.float32)  6.51 us
  transfers between devices with their start and end apart: 1, of which 1 were waited for; matrix products, arithmetic and copies ran while one was open for 8% of the time, Pallas kernels for 0%

commit v1 on v0

v1 whole, which is shorter than its diff:
```python
import functools
import math

import jax
import jax.numpy as jnp
from jax import lax
from jax.experimental import pallas as pl
from jax.experimental.pallas import tpu as pltpu
from jax.sharding import PartitionSpec as P

MESH = pl.DeviceIdType.MESH
BF = jnp.bfloat16
F32 = jnp.float32
CHUNKS = 8


def exact(a, b):
    return jnp.dot(a, b, precision=lax.Precision.HIGHEST, preferred_element_type=F32)


def exact_nt(a, b):
    return lax.dot_general(
        a, b, (((1,), (1,)), ((), ())), precision=lax.Precision.HIGHEST, preferred_element_type=F32
    )


def dot_nt(a, b):
    return lax.dot_general(a, b, (((1,), (1,)), ((), ())), preferred_element_type=F32)


def split(x):
    high = x.astype(BF)
    return high, (x - high.astype(F32)).astype(BF)


def iota(shape, axis):
    return lax.broadcasted_iota(jnp.int32, shape, axis)


def exchange(groups, spread, bins_ref, snap_ref, basis_ref, spec_ref, coef_ref, gram_ref,
             xs, ub, terms, recv, cbuf, gbuf, in_sem, rs_send, rs_recv, g_send, g_recv, c_send, c_recv):
    slice_len = snap_ref.shape[0]
    points = snap_ref.shape[2]
    nb, _, rank = basis_ref.shape[:3]
    nbins = bins_ref.shape[0]
    rows = 4 * rank
    step = points // CHUNKS
    total = slice_len * groups
    me_t = lax.axis_index("ta")
    me_s = lax.axis_index("sa")
    loads = [
        pltpu.make_async_copy(
            snap_ref.at[:, v, pl.ds(h * (points // 2), points // 2)],
            xs.at[v, :, pl.ds(h * (points // 2), points // 2)], in_sem.at[2 * h + v])
        for h in range(2) for v in range(2)
    ]
    for load in loads:
        load.start()
    load_basis = pltpu.make_async_copy(
        basis_ref.reshape(nb * rows, points), ub, in_sem.at[4])
    load_basis.start()

    barrier = pltpu.get_barrier_semaphore()
    for d in range(1, groups):
        pl.semaphore_signal(barrier, inc=1, device_id=(lax.rem(me_t + d, groups), me_s), device_id_type=MESH)
    for d in range(1, spread):
        pl.semaphore_signal(barrier, inc=1, device_id=(me_t, lax.rem(me_s + d, spread)), device_id_type=MESH)

    row = iota((2 * nbins, slice_len), 0)
    t = iota((2 * nbins, slice_len), 1) + me_t * slice_len
    bin_of = jnp.zeros((2 * nbins, slice_len), jnp.int32)
    for b in range(nbins):
        bin_of = jnp.where(row // 2 == b, bins_ref[b], bin_of)
    phase = jnp.bitwise_and(bin_of * t + (row % 2) * (total // 4), total - 1)
    unit = 2.0 * math.pi / total
    window = 0.5 - 0.5 * jnp.cos(unit * t.astype(F32))
    table = jnp.cos(unit * phase.astype(F32)) * window * math.sqrt(8.0 / (3.0 * total))
    th, tl = split(table)
    left = jnp.concatenate(
        [jnp.concatenate([th, th], axis=1), jnp.concatenate([tl, jnp.zeros_like(tl)], axis=1)], axis=0)

    pl.semaphore_wait(barrier, groups - 1 + spread - 1)

    sends = []
    for k in range(CHUNKS):
        if k == 0:
            loads[0].wait()
            loads[1].wait()
        if k == CHUNKS // 2:
            loads[2].wait()
            loads[3].wait()
        cols = pl.ds(k * step, step)
        for v in range(2):
            xh, xl = split(xs[v, :, cols])
            out = jnp.dot(left, jnp.concatenate([xh, xl], axis=0), preferred_element_type=F32)
            out = out[: 2 * nbins] + out[2 * nbins:]
            terms[:, v, :, cols] = out.reshape(groups, 2 * nb, step)
        for d in range(1, groups):
            peer = lax.rem(me_t + d, groups)
            copy = pltpu.make_async_remote_copy(
                src_ref=terms.at[peer, :, :, cols], dst_ref=recv.at[d - 1, :, :, cols],
                send_sem=rs_send.at[k, d - 1], recv_sem=rs_recv.at[k, d - 1],
                device_id=(peer, me_s), device_id_type=MESH)
            copy.start()
            sends.append(copy)

    load_basis.wait()
    ri, ci = iota((rows, rows), 0), iota((rows, rows), 1)
    same_v = (ri % 2) == (ci % 2)
    same_c = (ri // (2 * rank)) == (ci // (2 * rank))
    one = jnp.ones((rows, rows), F32)
    keep_re = jnp.where(jnp.logical_and(same_v, same_c), one, 0.0)
    keep_im = jnp.where(jnp.logical_and(same_v, jnp.logical_not(same_c)),
                        jnp.where(ri < 2 * rank, one, -one), 0.0)
    mode = (ri // 2) % rank
    fold = jnp.where(iota((rank, rows), 0) == (iota((rank, rows), 1) // 2) % rank, 1.0, 0.0)
    for p in range(nb // 2):
        wide = jnp.zeros((rows, rows), F32)
        for h in range(2):
            w = ub[pl.ds((2 * p + h) * rows, rows), :]
            m = dot_nt(w, w)
            wide += exact(m * keep_re, jnp.where(ci == mode + 2 * h * rank, 1.0, 0.0))
            wide += exact(m * keep_im, jnp.where(ci == mode + (2 * h + 1) * rank, 1.0, 0.0))
        gbuf[me_s, p] = exact(fold, wide)
    g_copies = []
    for d in range(1, spread):
        copy = pltpu.make_async_remote_copy(
            src_ref=gbuf.at[me_s], dst_ref=gbuf.at[me_s], send_sem=g_send.at[d], recv_sem=g_recv.at[d],
            device_id=(me_t, lax.rem(me_s + d, spread)), device_id_type=MESH)
        copy.start()
        g_copies.append(copy)

    acc = jnp.zeros((8 * nb, nb * rows), F32)
    square = jnp.zeros((2 * nb, 128), F32)
    for k in range(CHUNKS):
        cols = pl.ds(k * step, step)
        for d in range(1, groups):
            sends[k * (groups - 1) + d - 1].wait_recv()
        spec = terms[me_t, :, :, cols]
        for d in range(1, groups):
            spec = spec + recv[d - 1, :, :, cols]
        spec_ref[:, :, cols] = spec
        sq = spec[0] * spec[0] + spec[1] * spec[1]
        for i in range(step // 128):
            square = square + sq[:, i * 128:(i + 1) * 128]
        flat = spec.reshape(4 * nb, step)
        sh, sl = split(flat)
        acc = acc + dot_nt(jnp.concatenate([sh, sl], axis=0), ub[:, cols])
    ar, ac = iota(acc.shape, 0), iota(acc.shape, 1)
    match = jnp.logical_and((ar // 2) % nb == ac // rows, (ar // (2 * nb)) % 2 == ac % 2)
    c_col = (ac // (2 * rank)) % 2
    same = ar % 2 == c_col
    a_re = jnp.where(jnp.logical_and(match, same), acc, 0.0)
    a_im = jnp.where(jnp.logical_and(match, jnp.logical_not(same)), jnp.where(c_col == 0, acc, -acc), 0.0)
    qr, qc = iota((2 * nb, 8 * nb), 0), iota((2 * nb, 8 * nb), 1)
    q_bin = qr // 2 == (qc // 2) % nb
    q_re = jnp.where(jnp.logical_and(q_bin, qr % 2 == 0), 1.0, 0.0)
    q_im = jnp.where(jnp.logical_and(q_bin, qr % 2 == 1), 1.0, 0.0)
    er, ec = iota((nb * rows, 128), 0), iota((nb * rows, 128), 1)
    pick = jnp.where((er // 2) % rank == ec, 1.0, 0.0)
    coef = exact(exact(q_re, a_re) + exact(q_im, a_im), pick)
    norm = jnp.sum(square, axis=1, keepdims=True)
    cbuf[me_s] = jnp.where(iota((2 * nb, 128), 1) == rank, norm, coef)
    c_copies = []
    for d in range(1, spread):
        copy = pltpu.make_async_remote_copy(
            src_ref=cbuf.at[me_s], dst_ref=cbuf.at[me_s], send_sem=c_send.at[d], recv_sem=c_recv.at[d],
            device_id=(me_t, lax.rem(me_s + d, spread)), device_id_type=MESH)
        copy.start()
        c_copies.append(copy)
    for copy in g_copies:
        copy.wait_recv()
    gram = gbuf[0]
    for s in range(1, spread):
        gram = gram + gbuf[s]
    gram_ref[...] = gram
    for copy in c_copies:
        copy.wait_recv()
    coef = cbuf[0]
    for s in range(1, spread):
        coef = coef + cbuf[s]
    coef_ref[...] = coef
    for copy in sends + g_copies + c_copies:
        copy.wait_send()


def update(count_ref, eig_ref, coef_ref, gram_ref, spec_ref, basis_ref, fresh_ref, coh_ref, ub, ob, in_sem, out_sem):
    nb, _, rank = basis_ref.shape[:3]
    points = basis_ref.shape[4]
    rows = 4 * rank
    flat_in = basis_ref.reshape(nb * rows, points)
    flat_out = fresh_ref.reshape(nb * rows, points)
    loads = [pltpu.make_async_copy(flat_in.at[pl.ds(b * rows, rows), :], ub.at[pl.ds(b * rows, rows), :], in_sem.at[b])
             for b in range(nb)]
    stores = [pltpu.make_async_copy(ob.at[pl.ds(b * rows, rows), :], flat_out.at[pl.ds(b * rows, rows), :], out_sem.at[b])
              for b in range(nb)]
    for load in loads:
        load.start()
    count = jnp.full((1, 1), count_ref[0], jnp.int32).astype(F32)
    w_old = count / (count + 1.0)
    w_new = 1.0 / (count + 1.0)
    scaled = w_old * eig_ref[...]
    coef = coef_ref[...]
    coef_t = jnp.transpose(coef)
    scaled_t = jnp.transpose(jnp.concatenate([scaled, scaled], axis=0))
    eye = iota((rank, rank), 0) == iota((rank, rank), 1)
    r8 = iota((2 * nb, rank), 0)
    k_p = jnp.zeros((2 * nb, rank), F32)
    k_s = jnp.zeros((2 * nb, rank), F32)
    k_a = jnp.zeros((2 * nb, rank), F32)
    for b in range(nb):
        g = gram_ref[b // 2]
        at = 2 * rank * (b % 2)
        g_re, g_im = g[:, at:at + rank], g[:, at + rank:at + 2 * rank]
        cr, ci = coef[2 * b:2 * b + 1, :rank], coef[2 * b + 1:2 * b + 2, :rank]
        cr_c, ci_c = coef_t[:rank, 2 * b:2 * b + 1], coef_t[:rank, 2 * b + 1:2 * b + 2]
        norm = coef[2 * b:2 * b + 1, rank:rank + 1] + coef[2 * b + 1:2 * b + 2, rank:rank + 1]
        a, a_c = scaled[b:b + 1], scaled_t[:, b:b + 1]
        weight = w_new * (a_c + a) + (w_new * w_new) * norm
        pair = a_c * a
        full_re = pair * g_re + weight * (cr_c * cr + ci_c * ci)
        full_im = pair * g_im + weight * (ci_c * cr - cr_c * ci)
        diag = jnp.where(eye, full_re, 0.0)
        inv = 1.0 / jnp.sqrt(jnp.sum(diag, axis=0, keepdims=True) + 1e-06)
        inv_c = 1.0 / jnp.sqrt(jnp.sum(diag, axis=1, keepdims=True) + 1e-06)
        outer = inv_c * inv
        coh_ref[b, 0] = full_re * outer
        coh_ref[b, 1] = full_im * outer
        p_row, q_row = inv * w_new * cr, inv * w_new * ci
        k_p = jnp.where(r8 == 2 * b, p_row, jnp.where(r8 == 2 * b + 1, q_row, k_p))
        k_s = jnp.where(r8 == 2 * b, -q_row, jnp.where(r8 == 2 * b + 1, p_row, k_s))
        k_a = jnp.where(r8 == 2 * b, inv * a, k_a)
    wide = 12 * nb
    er, ec = iota((nb * rows, rank), 0), iota((nb * rows, rank), 1)
    pick = jnp.where((er // 2) % rank == ec, 1.0, 0.0)
    t_p = exact_nt(pick, jnp.concatenate([k_p] * 6, axis=0))
    t_s = exact_nt(pick, jnp.concatenate([k_s] * 6, axis=0))
    t_a = exact_nt(pick, k_a)
    rr, rc = iota((nb * rows, wide), 0), iota((nb * rows, wide), 1)
    match = jnp.logical_and(rr // rows == (rc // 2) % nb, rr % 2 == (rc // (2 * nb)) % 2)
    mix = jnp.where(match, jnp.where((rr // (2 * rank)) % 2 == 0, t_p, t_s), 0.0)
    mh = mix.astype(BF)
    left = jnp.where(rc < 8 * nb, mh.astype(F32), mix - mh.astype(F32)).astype(BF)
    r2, c2 = iota((nb * rows, 2 * nb), 0), iota((nb * rows, 2 * nb), 1)
    gain = jnp.sum(jnp.where(r2 // rows == c2 // 2, t_a, 0.0), axis=1, keepdims=True)
    sh, sl = split(spec_ref[...].reshape(4 * nb, points))
    right = jnp.concatenate([sh, sl, sh], axis=0)
    step = 512
    for b in range(nb):
        loads[b].wait()
        at = pl.ds(b * rows, rows)
        lb, gb = left[b * rows:(b + 1) * rows], gain[b * rows:(b + 1) * rows]
        for k in range(points // step):
            cols = pl.ds(k * step, step)
            add = jnp.dot(lb, right[:, k * step:(k + 1) * step], preferred_element_type=F32)
            ob[at, cols] = (gb * ub[at, cols].astype(F32) + add).astype(BF)
        stores[b].start()
    for store in stores:
        store.wait()


def local(groups, spread, snapshots, bins, eigenvalues, old_basis, block_count):
    slice_len, _, points = snapshots.shape
    nb, _, rank = old_basis.shape[:3]
    rows = 4 * rank
    vmem = pl.BlockSpec(memory_space=pltpu.VMEM)
    smem = pl.BlockSpec(memory_space=pltpu.SMEM)
    hbm = pl.BlockSpec(memory_space=pl.ANY)
    spec, coef, gram = pl.pallas_call(
        functools.partial(exchange, groups, spread),
        out_shape=(
            jax.ShapeDtypeStruct((2, 2 * nb, points), F32),
            jax.ShapeDtypeStruct((2 * nb, 128), F32),
            jax.ShapeDtypeStruct((nb // 2, rank, 128), F32),
        ),
        in_specs=[smem, hbm, hbm],
        out_specs=(vmem, vmem, vmem),
        scratch_shapes=[
            pltpu.VMEM((2, slice_len, points), F32),
            pltpu.VMEM((nb * rows, points), BF),
            pltpu.VMEM((groups, 2, 2 * nb, points), F32),
            pltpu.VMEM((groups - 1, 2, 2 * nb, points), F32),
            pltpu.VMEM((spread, 2 * nb, 128), F32),
            pltpu.VMEM((spread, nb // 2, rank, 128), F32),
            pltpu.SemaphoreType.DMA((5,)),
            pltpu.SemaphoreType.DMA((CHUNKS, groups - 1)),
            pltpu.SemaphoreType.DMA((CHUNKS, groups - 1)),
            pltpu.SemaphoreType.DMA((spread,)),
            pltpu.SemaphoreType.DMA((spread,)),
            pltpu.SemaphoreType.DMA((spread,)),
            pltpu.SemaphoreType.DMA((spread,)),
        ],
        compiler_params=pltpu.CompilerParams(
            collective_id=0, has_side_effects=True, vmem_limit_bytes=40 * 2**20),
        name="exchange",
    )(bins, snapshots, old_basis)
    fresh, coherence = pl.pallas_call(
        update,
        out_shape=(
            jax.ShapeDtypeStruct(old_basis.shape, BF),
            jax.ShapeDtypeStruct((nb, 2, rank, rank), F32),
        ),
        in_specs=[smem, vmem, vmem, vmem, vmem, hbm],
        out_specs=(hbm, vmem),
        scratch_shapes=[
            pltpu.VMEM((nb * rows, points), BF),
            pltpu.VMEM((nb * rows, points), BF),
            pltpu.SemaphoreType.DMA((nb,)),
            pltpu.SemaphoreType.DMA((nb,)),
        ],
        compiler_params=pltpu.CompilerParams(vmem_limit_bytes=40 * 2**20),
        name="update",
    )(block_count, eigenvalues, coef, gram, spec, old_basis)
    return fresh, coherence


def solution(mesh):
    groups, spread = mesh.shape["ta"], mesh.shape["sa"]
    return jax.shard_map(
        functools.partial(local, groups, spread),
        mesh=mesh,
        in_specs=(P("ta", None, "sa"), P(), P("ta", None), P("ta", None, None, None, "sa"), P()),
        out_specs=(P("ta", None, None, None, "sa"), P("ta", None, None, None)),
        check_vma=False,
    )
```

time: 200 us -> 42.3 us (0.21); the launches traced: 198 us -> 42.1 us
  matrix products: 53.8 us -> 0 us
  blocking collectives: 43.8 us -> 0 us
  waiting for transfers between devices: 39.1 us -> 0 us
  Pallas kernels: 0 us -> 36.3 us
  other arithmetic: 23.6 us -> 0 us
  local copies, waits for them, and re-layouts: 21.4 us -> 4.43 us
  between operations: 15.8 us -> 1.31 us
    dot_general x10 -> x0, matrix products: 53.8 us -> none  [the longest x8 51.5 us: pair_dot(): return jnp.einsum(form, left, right, precision=lax.Precision.HIGHEST)]
    psum x2 -> x0, blocking collectives: 43.8 us -> none  [the longest x1 27.2 us: local(): gram_re, gram_im = lax.psum((part_re, part_im), 'sa')]
    unnamed x2 -> x0, waiting for transfers between devices: 39.1 us -> none
    pallas_call x0 -> x2, Pallas kernels: none -> 36.3 us  [the longest x1 28.5 us: local(): pl.pallas_call(functools.partial(exchange, groups, spread), out_shape=(ja...]
    another operation x5 -> x0, other arithmetic: 17 us -> none  [the longest x1 10.4 us: local(): jnp.stack([g_re * inv[:, :, None], g_im * inv[:, :, None]], axis=1)]
    reshape x1 -> x0, local copies, waits for them, and re-layouts: 7.8 us -> none  [local(): old_basis.reshape(local_bins, 2, rank, 2 * points).astype(jnp.float32)]
    another operation x2 -> x0, local copies, waits for them, and re-layouts: 7.2 us -> none  [local(): jnp.stack([g_re * inv[:, :, None], g_im * inv[:, :, None]], axis=1)]
    convert_element_type x1 -> x0, other arithmetic: 6.51 us -> none  [local(): old_basis.reshape(local_bins, 2, rank, 2 * points).astype(jnp.float32)]
  transfers between devices with their start and end apart: 1 -> 0, of which waited for: 1 -> 0; matrix products, arithmetic and copies ran while one was open for 8% -> 0% of each run, Pallas kernels for 0% -> 0%
where the time goes in v1:
time: 42.3 us; the launch traced here: 42.1 us
  Pallas kernels  36.3 us (86%)
  local copies, waits for them, and re-layouts  4.43 us (10%)
  between operations  1.31 us (3%)
    pallas_call x1, Pallas kernels, local(): pl.pallas_call(functools.partial(exchange, groups, spread), out_shape=(ja...  28.5 us
    pallas_call x1, Pallas kernels, local(): pl.pallas_call(update, out_shape=(jax.ShapeDtypeStruct(old_basis.shape, B...  7.85 us
    unnamed x10, local copies, waits for them, and re-layouts  4.43 us

profile of v1, /device:TPU:0, one launch (start us, length us, event | category | flops | bytes accessed | tf_op | source)
XLA Modules:
  0.0 42.1 jit_solution(3775038908656962613)
XLA Ops:
  1.3 0.0 copy-start
  1.3 2.2 %copy-done = bf16[4,2,32,2,4096]{4,3,2,1,0:T(2,128)(2,1)S(1)} copy-done((bf16[4,2,32,2,4096]{4,3,2,1,0:T(2,128)(2,1)S(1)}, bf16[4,2,32,2,4096]{4,3,2,1,0:T(2,128)(2,1)}, u32[]{:S(2)}) %copy-start) | copy-done | bytes 4194328
  3.5 0.0 copy-start.2
  3.5 1.6 %copy-done.2 = f32[64,2,4096]{2,1,0:T(2,128)S(1)} copy-done((f32[64,2,4096]{2,1,0:T(2,128)S(1)}, f32[64,2,4096]{2,1,0:T(2,128)}, u32[]{:S(2)}) %copy-start.2) | copy-done | bytes 2097176
  5.1 0.0 copy-start.4
  5.1 0.7 %copy-done.4 = s32[16]{0:T(128)S(1)} copy-done((s32[16]{0:T(128)S(1)}, s32[16]{0:T(128)}, u32[]{:S(2)}) %copy-start.4) | copy-done | bytes 88
  5.7 0.0 copy-start.1
  5.7 0.0 copy-start.3
  5.7 28.5 %exchange.1 = (f32[2,8,4096]{2,1,0:T(8,128)S(1)}, f32[8,128]{1,0:T(8,128)S(1)}, f32[2,32,128]{2,1,0:T(8,128)S(1)}) custom-call(s32[16]{0:T(128)S(1)} %copy-done.4, f32[64,2,4096]{2,1,0:T(2,128)S(1)} %copy-done.2, bf16[4,2,32,2,4096]{4,3,2,1,0:T(2,128)(2,1)S(1)} %copy-done), custom_call_target="tpu_custom_call" | custom-call | tf_op jit(solution)/shard_map/exchange/pallas_call | solution.py:269
  34.2 0.0 copy-done.1
  34.2 0.0 copy-done.3
  34.2 7.8 %update.1 = (bf16[4,2,32,2,4096]{4,3,2,1,0:T(2,128)(2,1)}, f32[4,2,32,32]{3,2,1,0:T(8,128)}) custom-call(s32[1]{0:T(128)S(6)} %copy.7.count_ref, f32[4,32]{1,0:T(4,128)S(1)} %copy-done.3, f32[8,128]{1,0:T(8,128)S(1)} %get-tuple-element.5.coef_ref, f32[2,32,128]{2,1,0:T(8,128)S(1)} %get-tuple-element.6.gram_ref, f32[2,8,4096]{2,1,0:T(8,128)S(1)} %get-tuple-element.7.spec_ref, ...), custom_call_target="tpu_custom_call" | custom-call | tf_op jit(solution)/shard_map/update/pallas_call | solution.py:297
Async XLA Ops:
  1.3 2.2 %copy-start = (bf16[4,2,32,2,4096]{4,3,2,1,0:T(2,128)(2,1)S(1)}, bf16[4,2,32,2,4096]{4,3,2,1,0:T(2,128)(2,1)}, u32[]{:S(2)}) copy-start(bf16[4,2,32,2,4096]{4,3,2,1,0:T(2,128)(2,1)} %basis_ref.3) | copy-start | bytes 12582916
  3.5 1.6 %copy-start.2 = (f32[64,2,4096]{2,1,0:T(2,128)S(1)}, f32[64,2,4096]{2,1,0:T(2,128)}, u32[]{:S(2)}) copy-start(f32[64,2,4096]{2,1,0:T(2,128)} %snap_ref.1) | copy-start | bytes 6291460
  5.1 0.7 %copy-start.4 = (s32[16]{0:T(128)S(1)}, s32[16]{0:T(128)}, u32[]{:S(2)}) copy-start(s32[16]{0:T(128)} %bins_ref.1) | copy-start | bytes 196
  5.7 28.5 %copy-start.1 = (bf16[4,2,32,2,4096]{4,3,2,1,0:T(2,128)(2,1)S(1)}, bf16[4,2,32,2,4096]{4,3,2,1,0:T(2,128)(2,1)}, u32[]{:S(2)}) copy-start(bf16[4,2,32,2,4096]{4,3,2,1,0:T(2,128)(2,1)} %basis_ref.3) | copy-start | bytes 12582916
  5.7 28.5 %copy-start.3 = (f32[4,32]{1,0:T(4,128)S(1)}, f32[4,32]{1,0:T(4,128)}, u32[]{:S(2)}) copy-start(f32[4,32]{1,0:T(4,128)} %eig_ref.1) | copy-start | bytes 1540

commit v2 on v1

v2 whole, which is shorter than its diff:
```python
import functools
import math

import jax
import jax.numpy as jnp
from jax import lax
from jax.experimental import pallas as pl
from jax.experimental.pallas import tpu as pltpu
from jax.sharding import PartitionSpec as P

MESH = pl.DeviceIdType.MESH
BF = jnp.bfloat16
F32 = jnp.float32
CHUNKS = 8
LIMIT = 40 * 2**20


def dot_nt(a, b):
    return lax.dot_general(a, b, (((1,), (1,)), ((), ())), preferred_element_type=F32)


def split(x):
    high = x.astype(BF)
    return high, (x - high.astype(F32)).astype(BF)


def split3(x):
    high = x.astype(BF)
    rest = x - high.astype(F32)
    mid = rest.astype(BF)
    return high, mid, (rest - mid.astype(F32)).astype(BF)


def right_pick(x, pick):
    n = x.shape[0]
    out = jnp.dot(jnp.concatenate(split3(x), axis=0), pick, preferred_element_type=F32)
    return out[:n] + out[n:2 * n] + out[2 * n:]


def iota(shape, axis):
    return lax.broadcasted_iota(jnp.int32, shape, axis)


def ones_where(mask):
    return jnp.where(mask, 1.0, 0.0).astype(BF)


def exchange(groups, spread, bins_ref, snap_ref, basis_ref, spec_ref, coef_ref, gram_ref,
             bins, xs, ub, terms, recv, fwd, cbuf, gbuf, in_sem, rs_send, rs_recv, g_send, g_recv, c_send, c_recv):
    assert groups == 4
    slice_len = snap_ref.shape[0]
    points = snap_ref.shape[2]
    nb, _, rank = basis_ref.shape[:3]
    nbins = bins_ref.shape[0]
    rows = 4 * rank
    step = points // CHUNKS
    total = slice_len * groups
    me_t = lax.axis_index("ta")
    me_s = lax.axis_index("sa")
    load_bins = pltpu.make_async_copy(bins_ref, bins, in_sem.at[5])
    load_bins.start()
    loads = [
        pltpu.make_async_copy(
            snap_ref.at[:, v, pl.ds(h * (points // 2), points // 2)],
            xs.at[v, :, pl.ds(h * (points // 2), points // 2)], in_sem.at[2 * h + v])
        for h in range(2) for v in range(2)
    ]
    for load in loads:
        load.start()
    load_basis = pltpu.make_async_copy(
        basis_ref.reshape(nb * rows, points), ub, in_sem.at[4])
    load_basis.start()

    near = me_t + 1 - 2 * lax.rem(me_t, 2)
    far = lax.rem(me_t + 2, 4)
    diagonal = lax.rem(near + 2, 4)
    barrier = pltpu.get_barrier_semaphore()
    for peer in (near, far):
        pl.semaphore_signal(barrier, inc=1, device_id=(peer, me_s), device_id_type=MESH)
    for d in range(1, spread):
        pl.semaphore_signal(barrier, inc=1, device_id=(me_t, lax.rem(me_s + d, spread)), device_id_type=MESH)

    t = iota((2 * nbins, slice_len), 1) + me_t * slice_len
    row = iota((2 * nbins, slice_len), 0)
    unit = 2.0 * math.pi / total
    window = (0.5 - 0.5 * jnp.cos(unit * t[:8].astype(F32))) * math.sqrt(8.0 / (3.0 * total))
    window = jnp.concatenate([window] * (2 * nbins // 8), axis=0)
    load_bins.wait()
    bin_of = jnp.zeros((2 * nbins, slice_len), jnp.int32)
    for b in range(nbins):
        bin_of = jnp.where(row // 2 == b, bins[b], bin_of)
    phase = jnp.bitwise_and(bin_of * t + (row % 2) * (total // 4), total - 1)
    th, tl = split(jnp.cos(unit * phase.astype(F32)) * window)
    left = jnp.concatenate(
        [jnp.concatenate([th, th], axis=1), jnp.concatenate([tl, jnp.zeros_like(tl)], axis=1)], axis=0)

    pl.semaphore_wait(barrier, 2 + spread - 1)

    def rs_copy(src, slot, v, k, peer):
        cols = pl.ds(k * step, step)
        return pltpu.make_async_remote_copy(
            src_ref=src.at[v, :, cols], dst_ref=recv.at[slot, v, :, cols],
            send_sem=rs_send.at[k, v, slot], recv_sem=rs_recv.at[k, v, slot],
            device_id=(peer, me_s), device_id_type=MESH)

    first, second = (near, far), (far, near)
    copies = {}
    for k in range(CHUNKS):
        if k == 0:
            loads[0].wait()
            loads[1].wait()
        if k == CHUNKS // 2:
            loads[2].wait()
            loads[3].wait()
        cols = pl.ds(k * step, step)
        for v in range(2):
            xh, xl = split(xs[v, :, cols])
            out = jnp.dot(left, jnp.concatenate([xh, xl], axis=0), preferred_element_type=F32)
            out = out[: 2 * nbins] + out[2 * nbins:]
            terms[:, v, :, cols] = out.reshape(groups, 2 * nb, step)
            copies[k, v, 0] = rs_copy(terms.at[diagonal], 0, v, k, first[v])
            copies[k, v, 1] = rs_copy(terms.at[first[v]], 1, v, k, first[v])
            copies[k, v, 0].start()
            copies[k, v, 1].start()

    def pass_on(k):
        cols = pl.ds(k * step, step)
        for v in range(2):
            copies[k, v, 0].wait_recv()
            fwd[v, :, cols] = terms[second[v], v, :, cols] + recv[0, v, :, cols]
            copies[k, v, 2] = rs_copy(fwd, 2, v, k, second[v])
            copies[k, v, 2].start()

    load_basis.wait()
    two = 2 * rows
    ri, ci = iota((two, two), 0), iota((two, two), 1)
    same_v = jnp.logical_and((ri % 2) == (ci % 2), ri // rows == ci // rows)
    r_c, c_c = (ri // (2 * rank)) % 2, (ci // (2 * rank)) % 2
    keep_re = jnp.where(jnp.logical_and(same_v, r_c == c_c), 1.0, 0.0)
    keep_im = jnp.where(jnp.logical_and(same_v, r_c != c_c), jnp.where(r_c == 0, 1.0, -1.0), 0.0)
    pr, pc = iota((2 * two, 128), 0), iota((2 * two, 128), 1)
    place = ones_where(pc == (pr // 2) % rank + 2 * rank * ((pr // rows) % 2) + rank * (pr // two))
    fold = ones_where(iota((rank, 3 * two), 0) == (iota((rank, 3 * two), 1) // 2) % rank)
    for p in range(nb // 2):
        w = ub[pl.ds(p * two, two), :]
        big = dot_nt(w, w)
        for k in range(p * CHUNKS // nb, (p + 1) * CHUNKS // nb):
            pass_on(k)
        wide = right_pick(jnp.concatenate([big * keep_re, big * keep_im], axis=1), place)
        gbuf[me_s, p] = jnp.dot(fold, jnp.concatenate(split3(wide), axis=0), preferred_element_type=F32)
    g_copies = []
    for d in range(1, spread):
        copy = pltpu.make_async_remote_copy(
            src_ref=gbuf.at[me_s], dst_ref=gbuf.at[me_s], send_sem=g_send.at[d], recv_sem=g_recv.at[d],
            device_id=(me_t, lax.rem(me_s + d, spread)), device_id_type=MESH)
        copy.start()
        g_copies.append(copy)
    for k in range((nb // 2) * CHUNKS // nb, CHUNKS):
        pass_on(k)

    er, ec = iota((nb * rows, 128), 0), iota((nb * rows, 128), 1)
    pick = ones_where((er // 2) % rank == ec)
    acc = jnp.zeros((8 * nb, nb * rows), F32)
    square = jnp.zeros((2 * nb, 128), F32)
    for k in range(CHUNKS):
        cols = pl.ds(k * step, step)
        for v in range(2):
            copies[k, v, 1].wait_recv()
            copies[k, v, 2].wait_recv()
        spec = terms[me_t, :, :, cols] + recv[1, :, :, cols] + recv[2, :, :, cols]
        sq = spec[0] * spec[0] + spec[1] * spec[1]
        for i in range(step // 128):
            square = square + sq[:, i * 128:(i + 1) * 128]
        both = jnp.concatenate(split(spec.reshape(4 * nb, step)), axis=0)
        spec_ref[:, cols] = both
        acc = acc + dot_nt(both, ub[:, cols])
    acc = acc[: 4 * nb] + acc[4 * nb:]
    ar, ac = iota((2 * nb, nb * rows), 0), iota((2 * nb, nb * rows), 1)
    acc = jnp.where(ac % 2 == 0, acc[: 2 * nb], acc[2 * nb:])
    even = ar % 2 == 0
    other = jnp.where(even, pltpu.roll(acc, 2 * nb - 1, 0), -pltpu.roll(acc, 1, 0))
    acc = jnp.where((ac // (2 * rank)) % 2 == 0, acc, other)
    coef = right_pick(jnp.where(ar // 2 == ac // rows, acc, 0.0), pick)
    norm = jnp.sum(square, axis=1, keepdims=True)
    cbuf[me_s] = jnp.where(iota((2 * nb, 128), 1) == rank, norm, coef)
    c_copies = []
    for d in range(1, spread):
        copy = pltpu.make_async_remote_copy(
            src_ref=cbuf.at[me_s], dst_ref=cbuf.at[me_s], send_sem=c_send.at[d], recv_sem=c_recv.at[d],
            device_id=(me_t, lax.rem(me_s + d, spread)), device_id_type=MESH)
        copy.start()
        c_copies.append(copy)
    for copy in g_copies:
        copy.wait_recv()
    gram = gbuf[0]
    for s in range(1, spread):
        gram = gram + gbuf[s]
    gram_ref[...] = gram
    for copy in list(copies.values()) + g_copies:
        copy.wait_send()
    for copy in c_copies:
        copy.wait_recv()
    coef = cbuf[0]
    for s in range(1, spread):
        coef = coef + cbuf[s]
    coef_ref[...] = coef
    for copy in c_copies:
        copy.wait_send()


def update(count_ref, eig_ref, coef_ref, gram_ref, spec_ref, basis_ref, fresh_ref, coh_ref, ub, ob, in_sem, out_sem):
    nb, _, rank = basis_ref.shape[:3]
    points = basis_ref.shape[4]
    rows = 4 * rank
    flat_in = basis_ref.reshape(nb * rows, points)
    flat_out = fresh_ref.reshape(nb * rows, points)
    step = points // CHUNKS
    parts = [pl.ds(k * step, step) for k in range(CHUNKS)]
    loads = [pltpu.make_async_copy(flat_in.at[:, p], ub.at[:, p], in_sem.at[k]) for k, p in enumerate(parts)]
    stores = [pltpu.make_async_copy(ob.at[:, p], flat_out.at[:, p], out_sem.at[k]) for k, p in enumerate(parts)]
    for load in loads:
        load.start()
    count = jnp.full((1, 1), count_ref[0], jnp.int32).astype(F32)
    w_old = count / (count + 1.0)
    w_new = 1.0 / (count + 1.0)
    scaled = w_old * eig_ref[...]
    coef = coef_ref[...]
    coef_t = jnp.transpose(coef)
    scaled_t = jnp.transpose(jnp.concatenate([scaled, scaled], axis=0))
    eye = iota((rank, rank), 0) == iota((rank, rank), 1)
    r8 = iota((2 * nb, 128), 0)
    k_p = jnp.zeros((2 * nb, 128), F32)
    k_s = jnp.zeros((2 * nb, 128), F32)
    k_a = jnp.zeros((2 * nb, 128), F32)
    pad = jnp.zeros((1, 128 - rank), F32)
    for b in range(nb):
        g = gram_ref[b // 2]
        at = 2 * rank * (b % 2)
        g_re, g_im = g[:, at:at + rank], g[:, at + rank:at + 2 * rank]
        cr, ci = coef[2 * b:2 * b + 1, :rank], coef[2 * b + 1:2 * b + 2, :rank]
        cr_c, ci_c = coef_t[:rank, 2 * b:2 * b + 1], coef_t[:rank, 2 * b + 1:2 * b + 2]
        norm = coef[2 * b:2 * b + 1, rank:rank + 1] + coef[2 * b + 1:2 * b + 2, rank:rank + 1]
        a, a_c = scaled[b:b + 1], scaled_t[:, b:b + 1]
        weight = w_new * (a_c + a) + (w_new * w_new) * norm
        pair = a_c * a
        full_re = pair * g_re + weight * (cr_c * cr + ci_c * ci)
        full_im = pair * g_im + weight * (ci_c * cr - cr_c * ci)
        diag = jnp.where(eye, full_re, 0.0)
        inv = 1.0 / jnp.sqrt(jnp.sum(diag, axis=0, keepdims=True) + 1e-06)
        inv_c = 1.0 / jnp.sqrt(jnp.sum(diag, axis=1, keepdims=True) + 1e-06)
        outer = inv_c * inv
        coh_ref[b, 0] = full_re * outer
        coh_ref[b, 1] = full_im * outer
        p_row = jnp.concatenate([inv * w_new * cr, pad], axis=1)
        q_row = jnp.concatenate([inv * w_new * ci, pad], axis=1)
        a_row = jnp.concatenate([inv * a, pad], axis=1)
        k_p = jnp.where(r8 == 2 * b, p_row, jnp.where(r8 == 2 * b + 1, q_row, k_p))
        k_s = jnp.where(r8 == 2 * b, -q_row, jnp.where(r8 == 2 * b + 1, p_row, k_s))
        k_a = jnp.where(r8 == 2 * b, a_row, k_a)
    wide = 12 * nb
    lane = iota((2 * nb, 128), 1)
    k_mix = jnp.where(lane < rank, k_p, pltpu.roll(k_s, rank, 1))
    k_gain = jnp.where(lane < rank, k_a, pltpu.roll(k_a, rank, 1))
    er, ec = iota((nb * rows, 128), 0), iota((nb * rows, 128), 1)
    pick = ones_where((er // 2) % (2 * rank) == ec)
    values = jnp.concatenate([k_mix] * 6 + [k_gain], axis=0)
    spread_out = dot_nt(jnp.concatenate([pick] * 3, axis=1), jnp.concatenate(split3(values), axis=1))
    rr, rc = iota(spread_out.shape, 0), iota(spread_out.shape, 1)
    match = rr // rows == (rc // 2) % nb
    gain = jnp.sum(jnp.where(jnp.logical_and(match, jnp.logical_and(rc >= wide, rc % 2 == 0)), spread_out, 0.0),
                   axis=1, keepdims=True)
    match = jnp.logical_and(match, rr % 2 == (rc // (2 * nb)) % 2)
    mix = jnp.where(match, spread_out, 0.0)[:, :wide]
    mh = mix.astype(BF).astype(F32)
    left = jnp.where(rc[:, :wide] < 8 * nb, mh, mix - mh).astype(BF)
    for k, cols in enumerate(parts):
        right = jnp.concatenate([spec_ref[:, cols], spec_ref[: 4 * nb, cols]], axis=0)
        add = jnp.dot(left, right, preferred_element_type=F32)
        loads[k].wait()
        ob[:, cols] = (gain * ub[:, cols].astype(F32) + add).astype(BF)
        stores[k].start()
    for store in stores:
        store.wait()


def local(groups, spread, snapshots, bins, eigenvalues, old_basis, block_count):
    slice_len, _, points = snapshots.shape
    nb, _, rank = old_basis.shape[:3]
    rows = 4 * rank
    vmem = pl.BlockSpec(memory_space=pltpu.VMEM)
    smem = pl.BlockSpec(memory_space=pltpu.SMEM)
    hbm = pl.BlockSpec(memory_space=pl.ANY)
    spec, coef, gram = pl.pallas_call(
        functools.partial(exchange, groups, spread),
        out_shape=(
            jax.ShapeDtypeStruct((8 * nb, points), BF),
            jax.ShapeDtypeStruct((2 * nb, 128), F32),
            jax.ShapeDtypeStruct((nb // 2, rank, 128), F32),
        ),
        in_specs=[pl.BlockSpec(memory_space=pltpu.HBM)] * 3,
        out_specs=(vmem, vmem, vmem),
        scratch_shapes=[
            pltpu.SMEM(bins.shape, jnp.int32),
            pltpu.VMEM((2, slice_len, points), F32),
            pltpu.VMEM((nb * rows, points), BF),
            pltpu.VMEM((groups, 2, 2 * nb, points), F32),
            pltpu.VMEM((3, 2, 2 * nb, points), F32),
            pltpu.VMEM((2, 2 * nb, points), F32),
            pltpu.VMEM((spread, 2 * nb, 128), F32),
            pltpu.VMEM((spread, nb // 2, rank, 128), F32),
            pltpu.SemaphoreType.DMA((6,)),
            pltpu.SemaphoreType.DMA((CHUNKS, 2, 3)),
            pltpu.SemaphoreType.DMA((CHUNKS, 2, 3)),
            pltpu.SemaphoreType.DMA((spread,)),
            pltpu.SemaphoreType.DMA((spread,)),
            pltpu.SemaphoreType.DMA((spread,)),
            pltpu.SemaphoreType.DMA((spread,)),
        ],
        compiler_params=pltpu.CompilerParams(
            collective_id=0, has_side_effects=True, vmem_limit_bytes=LIMIT),
        name="exchange",
    )(*(pltpu.with_memory_space_constraint(x, pltpu.HBM) for x in (bins, snapshots, old_basis)))
    fresh, coherence = pl.pallas_call(
        update,
        out_shape=(
            jax.ShapeDtypeStruct(old_basis.shape, BF),
            jax.ShapeDtypeStruct((nb, 2, rank, rank), F32),
        ),
        in_specs=[smem, vmem, vmem, vmem, vmem, hbm],
        out_specs=(hbm, vmem),
        scratch_shapes=[
            pltpu.VMEM((nb * rows, points), BF),
            pltpu.VMEM((nb * rows, points), BF),
            pltpu.SemaphoreType.DMA((CHUNKS,)),
            pltpu.SemaphoreType.DMA((CHUNKS,)),
        ],
        compiler_params=pltpu.CompilerParams(vmem_limit_bytes=40 * 2**20),
        name="update",
    )(block_count, eigenvalues, coef, gram, spec, old_basis)
    return fresh, coherence


def solution(mesh):
    groups, spread = mesh.shape["ta"], mesh.shape["sa"]
    return jax.shard_map(
        functools.partial(local, groups, spread),
        mesh=mesh,
        in_specs=(P("ta", None, "sa"), P(), P("ta", None), P("ta", None, None, None, "sa"), P()),
        out_specs=(P("ta", None, None, None, "sa"), P("ta", None, None, None)),
        check_vma=False,
    )
```

time: 42.3 us -> 32.5 us (0.77)
  Pallas kernels: 36.3 us -> 30.8 us
  local copies, waits for them, and re-layouts: 4.43 us -> 0.01 us
    pallas_call x1, Pallas kernels: 28.5 us -> 21.6 us  [local(): pl.pallas_call(functools.partial(exchange, groups, spread), out_shape=(ja...]
    unnamed x10 -> x4, local copies, waits for them, and re-layouts: 4.43 us -> 0.01 us
    pallas_call x1, Pallas kernels: 7.85 us -> 9.2 us  [local(): pl.pallas_call(update, out_shape=(jax.ShapeDtypeStruct(old_basis.shape, B...]
where the time goes in v2:
time: 32.5 us; the launch traced here: 32.3 us
  Pallas kernels  30.8 us (95%)
  between operations  1.47 us (5%)
    pallas_call x1, Pallas kernels, local(): pl.pallas_call(functools.partial(exchange, groups, spread), out_shape=(ja...  21.6 us
    pallas_call x1, Pallas kernels, local(): pl.pallas_call(update, out_shape=(jax.ShapeDtypeStruct(old_basis.shape, B...  9.2 us

profile of v2, /device:TPU:0, one launch (start us, length us, event | category | flops | bytes accessed | tf_op | source)
XLA Modules:
  0.0 32.3 jit_solution(3681606329123516297)
XLA Ops:
  0.6 0.0 copy-start
  0.6 0.0 copy-start.1
  1.4 21.6 %exchange.1 = (bf16[32,4096]{1,0:T(8,128)(2,1)S(1)}, f32[8,128]{1,0:T(8,128)S(1)}, f32[2,32,128]{2,1,0:T(8,128)S(1)}) custom-call(s32[16]{0:T(128)} %bins_ref.1, f32[64,2,4096]{2,1,0:T(2,128)} %snap_ref.1, bf16[4,2,32,2,4096]{4,3,2,1,0:T(2,128)(2,1)} %basis_ref.3), custom_call_target="tpu_custom_call" | custom-call | tf_op jit(solution)/shard_map/exchange/pallas_call | solution.py:293
  23.1 0.0 copy-done
  23.1 0.0 copy-done.1
  23.1 9.2 %update.1 = (bf16[4,2,32,2,4096]{4,3,2,1,0:T(2,128)(2,1)}, f32[4,2,32,32]{3,2,1,0:T(8,128)}) custom-call(s32[1]{0:T(128)S(6)} %copy.7.count_ref, f32[4,32]{1,0:T(4,128)S(1)} %copy-done.1, f32[8,128]{1,0:T(8,128)S(1)} %get-tuple-element.5.coef_ref, f32[2,32,128]{2,1,0:T(8,128)S(1)} %get-tuple-element.6.gram_ref, ...), custom_call_target="tpu_custom_call" | custom-call | tf_op jit(solution)/shard_map/update/pallas_call | solution.py:323
Async XLA Ops:
  0.6 22.5 %copy-start = (bf16[4,2,32,2,4096]{4,3,2,1,0:T(2,128)(2,1)S(1)}, bf16[4,2,32,2,4096]{4,3,2,1,0:T(2,128)(2,1)}, u32[]{:S(2)}) copy-start(bf16[4,2,32,2,4096]{4,3,2,1,0:T(2,128)(2,1)} %basis_ref.3) | copy-start | bytes 12582916
  0.6 22.5 %copy-start.1 = (f32[4,32]{1,0:T(4,128)S(1)}, f32[4,32]{1,0:T(4,128)}, u32[]{:S(2)}) copy-start(f32[4,32]{1,0:T(4,128)} %eig_ref.1) | copy-start | bytes 1540

commit v3 on v2

--- a/solution.py
+++ b/solution.py
@@ -41,12 +41,22 @@
     return lax.broadcasted_iota(jnp.int32, shape, axis)
 
 
+def div(x, n):
+    assert n & (n - 1) == 0
+    return lax.shift_right_logical(x, jnp.full(x.shape, n.bit_length() - 1, x.dtype))
+
+
+def mod(x, n):
+    assert n & (n - 1) == 0
+    return jnp.bitwise_and(x, n - 1)
+
+
 def ones_where(mask):
     return jnp.where(mask, 1.0, 0.0).astype(BF)
 
 
-def exchange(groups, spread, bins_ref, snap_ref, basis_ref, spec_ref, coef_ref, gram_ref,
-             bins, xs, ub, terms, recv, fwd, cbuf, gbuf, in_sem, rs_send, rs_recv, g_send, g_recv, c_send, c_recv):
+def exchange(groups, spread, bins_ref, snap_ref, basis_ref, spec_ref, coef_ref, gram_ref, ub,
+             bins, xs, terms, recv, fwd, cbuf, gbuf, in_sem, b_sem, rs_send, rs_recv, g_send, g_recv, c_send, c_recv):
     assert groups == 4
     slice_len = snap_ref.shape[0]
     points = snap_ref.shape[2]
@@ -57,19 +67,17 @@
     total = slice_len * groups
     me_t = lax.axis_index("ta")
     me_s = lax.axis_index("sa")
-    load_bins = pltpu.make_async_copy(bins_ref, bins, in_sem.at[5])
+    load_bins = pltpu.make_async_copy(bins_ref, bins, b_sem.at[2 * nb])
     load_bins.start()
-    loads = [
-        pltpu.make_async_copy(
-            snap_ref.at[:, v, pl.ds(h * (points // 2), points // 2)],
-            xs.at[v, :, pl.ds(h * (points // 2), points // 2)], in_sem.at[2 * h + v])
-        for h in range(2) for v in range(2)
-    ]
-    for load in loads:
-        load.start()
-    load_basis = pltpu.make_async_copy(
-        basis_ref.reshape(nb * rows, points), ub, in_sem.at[4])
-    load_basis.start()
+    parts = [pl.ds(k * step, step) for k in range(CHUNKS)]
+    loads = [[pltpu.make_async_copy(snap_ref.at[:, v, p], xs.at[v, :, p], in_sem.at[v, k]) for v in range(2)]
+             for k, p in enumerate(parts)]
+    for pair in loads:
+        for load in pair:
+            load.start()
+    flat = basis_ref.reshape(nb * rows, points)
+    halves = [pl.ds(h * 2 * rank, 2 * rank) for h in range(2 * nb)]
+    load_basis = [pltpu.make_async_copy(flat.at[h], ub.at[h], b_sem.at[i]) for i, h in enumerate(halves)]
 
     near = me_t + 1 - 2 * lax.rem(me_t, 2)
     far = lax.rem(me_t + 2, 4)
@@ -88,8 +96,8 @@
     load_bins.wait()
     bin_of = jnp.zeros((2 * nbins, slice_len), jnp.int32)
     for b in range(nbins):
-        bin_of = jnp.where(row // 2 == b, bins[b], bin_of)
-    phase = jnp.bitwise_and(bin_of * t + (row % 2) * (total // 4), total - 1)
+        bin_of = jnp.where(div(row, 2) == b, bins[b], bin_of)
+    phase = jnp.bitwise_and(bin_of * t + mod(row, 2) * (total // 4), total - 1)
     th, tl = split(jnp.cos(unit * phase.astype(F32)) * window)
     left = jnp.concatenate(
         [jnp.concatenate([th, th], axis=1), jnp.concatenate([tl, jnp.zeros_like(tl)], axis=1)], axis=0)
@@ -106,14 +114,9 @@
     first, second = (near, far), (far, near)
     copies = {}
     for k in range(CHUNKS):
-        if k == 0:
-            loads[0].wait()
-            loads[1].wait()
-        if k == CHUNKS // 2:
-            loads[2].wait()
-            loads[3].wait()
-        cols = pl.ds(k * step, step)
+        cols = parts[k]
         for v in range(2):
+            loads[k][v].wait()
             xh, xl = split(xs[v, :, cols])
             out = jnp.dot(left, jnp.concatenate([xh, xl], axis=0), preferred_element_type=F32)
             out = out[: 2 * nbins] + out[2 * nbins:]
@@ -122,6 +125,9 @@
             copies[k, v, 1] = rs_copy(terms.at[first[v]], 1, v, k, first[v])
             copies[k, v, 0].start()
             copies[k, v, 1].start()
+        if k == 1:
+            for load in load_basis:
+                load.start()
 
     def pass_on(k):
         cols = pl.ds(k * step, step)
@@ -131,17 +137,18 @@
             copies[k, v, 2] = rs_copy(fwd, 2, v, k, second[v])
             copies[k, v, 2].start()
 
-    load_basis.wait()
     two = 2 * rows
     ri, ci = iota((two, two), 0), iota((two, two), 1)
-    same_v = jnp.logical_and((ri % 2) == (ci % 2), ri // rows == ci // rows)
-    r_c, c_c = (ri // (2 * rank)) % 2, (ci // (2 * rank)) % 2
+    same_v = mod(ri, 2) + 2 * div(ri, rows) == mod(ci, 2) + 2 * div(ci, rows)
+    r_c, c_c = mod(div(ri, 2 * rank), 2), mod(div(ci, 2 * rank), 2)
     keep_re = jnp.where(jnp.logical_and(same_v, r_c == c_c), 1.0, 0.0)
     keep_im = jnp.where(jnp.logical_and(same_v, r_c != c_c), jnp.where(r_c == 0, 1.0, -1.0), 0.0)
     pr, pc = iota((2 * two, 128), 0), iota((2 * two, 128), 1)
-    place = ones_where(pc == (pr // 2) % rank + 2 * rank * ((pr // rows) % 2) + rank * (pr // two))
-    fold = ones_where(iota((rank, 3 * two), 0) == (iota((rank, 3 * two), 1) // 2) % rank)
+    place = ones_where(pc == mod(div(pr, 2), rank) + 2 * rank * mod(div(pr, rows), 2) + rank * div(pr, two))
+    fold = ones_where(iota((rank, 3 * two), 0) == mod(div(iota((rank, 3 * two), 1), 2), rank))
     for p in range(nb // 2):
+        for load in load_basis[4 * p:4 * p + 4]:
+            load.wait()
         w = ub[pl.ds(p * two, two), :]
         big = dot_nt(w, w)
         for k in range(p * CHUNKS // nb, (p + 1) * CHUNKS // nb):
@@ -159,7 +166,7 @@
         pass_on(k)
 
     er, ec = iota((nb * rows, 128), 0), iota((nb * rows, 128), 1)
-    pick = ones_where((er // 2) % rank == ec)
+    pick = ones_where(mod(div(er, 2), rank) == ec)
     acc = jnp.zeros((8 * nb, nb * rows), F32)
     square = jnp.zeros((2 * nb, 128), F32)
     for k in range(CHUNKS):
@@ -176,11 +183,11 @@
         acc = acc + dot_nt(both, ub[:, cols])
     acc = acc[: 4 * nb] + acc[4 * nb:]
     ar, ac = iota((2 * nb, nb * rows), 0), iota((2 * nb, nb * rows), 1)
-    acc = jnp.where(ac % 2 == 0, acc[: 2 * nb], acc[2 * nb:])
-    even = ar % 2 == 0
+    acc = jnp.where(mod(ac, 2) == 0, acc[: 2 * nb], acc[2 * nb:])
+    even = mod(ar, 2) == 0
     other = jnp.where(even, pltpu.roll(acc, 2 * nb - 1, 0), -pltpu.roll(acc, 1, 0))
-    acc = jnp.where((ac // (2 * rank)) % 2 == 0, acc, other)
-    coef = right_pick(jnp.where(ar // 2 == ac // rows, acc, 0.0), pick)
+    acc = jnp.where(mod(div(ac, 2 * rank), 2) == 0, acc, other)
+    coef = right_pick(jnp.where(div(ar, 2) == div(ac, rows), acc, 0.0), pick)
     norm = jnp.sum(square, axis=1, keepdims=True)
     cbuf[me_s] = jnp.where(iota((2 * nb, 128), 1) == rank, norm, coef)
     c_copies = []
@@ -208,18 +215,13 @@
         copy.wait_send()
 
 
-def update(count_ref, eig_ref, coef_ref, gram_ref, spec_ref, basis_ref, fresh_ref, coh_ref, ub, ob, in_sem, out_sem):
-    nb, _, rank = basis_ref.shape[:3]
-    points = basis_ref.shape[4]
+def update(count_ref, eig_ref, coef_ref, gram_ref, spec_ref, ub, fresh_ref, coh_ref, ob, out_sem):
+    nb, _, rank = fresh_ref.shape[:3]
+    points = fresh_ref.shape[4]
     rows = 4 * rank
-    flat_in = basis_ref.reshape(nb * rows, points)
     flat_out = fresh_ref.reshape(nb * rows, points)
-    step = points // CHUNKS
-    parts = [pl.ds(k * step, step) for k in range(CHUNKS)]
-    loads = [pltpu.make_async_copy(flat_in.at[:, p], ub.at[:, p], in_sem.at[k]) for k, p in enumerate(parts)]
-    stores = [pltpu.make_async_copy(ob.at[:, p], flat_out.at[:, p], out_sem.at[k]) for k, p in enumerate(parts)]
-    for load in loads:
-        load.start()
+    halves = [pl.ds(h * 2 * rank, 2 * rank) for h in range(2 * nb)]
+    stores = [pltpu.make_async_copy(ob.at[h], flat_out.at[h], out_sem.at[i]) for i, h in enumerate(halves)]
     count = jnp.full((1, 1), count_ref[0], jnp.int32).astype(F32)
     w_old = count / (count + 1.0)
     w_new = 1.0 / (count + 1.0)
@@ -262,23 +264,27 @@
     k_mix = jnp.where(lane < rank, k_p, pltpu.roll(k_s, rank, 1))
     k_gain = jnp.where(lane < rank, k_a, pltpu.roll(k_a, rank, 1))
     er, ec = iota((nb * rows, 128), 0), iota((nb * rows, 128), 1)
-    pick = ones_where((er // 2) % (2 * rank) == ec)
+    pick = ones_where(mod(div(er, 2), 2 * rank) == ec)
     values = jnp.concatenate([k_mix] * 6 + [k_gain], axis=0)
     spread_out = dot_nt(jnp.concatenate([pick] * 3, axis=1), jnp.concatenate(split3(values), axis=1))
     rr, rc = iota(spread_out.shape, 0), iota(spread_out.shape, 1)
-    match = rr // rows == (rc // 2) % nb
-    gain = jnp.sum(jnp.where(jnp.logical_and(match, jnp.logical_and(rc >= wide, rc % 2 == 0)), spread_out, 0.0),
+    match = div(rr, rows) == mod(div(rc, 2), nb)
+    gain = jnp.sum(jnp.where(jnp.logical_and(match, jnp.logical_and(rc >= wide, mod(rc, 2) == 0)), spread_out, 0.0),
                    axis=1, keepdims=True)
-    match = jnp.logical_and(match, rr % 2 == (rc // (2 * nb)) % 2)
+    match = jnp.logical_and(match, mod(rr, 2) == mod(div(rc, 2 * nb), 2))
     mix = jnp.where(match, spread_out, 0.0)[:, :wide]
     mh = mix.astype(BF).astype(F32)
     left = jnp.where(rc[:, :wide] < 8 * nb, mh, mix - mh).astype(BF)
-    for k, cols in enumerate(parts):
-        right = jnp.concatenate([spec_ref[:, cols], spec_ref[: 4 * nb, cols]], axis=0)
-        add = jnp.dot(left, right, preferred_element_type=F32)
-        loads[k].wait()
-        ob[:, cols] = (gain * ub[:, cols].astype(F32) + add).astype(BF)
-        stores[k].start()
+    step = 512
+    for i, h in enumerate(halves):
+        at = i * 2 * rank
+        lh, gh = left[at:at + 2 * rank], gain[at:at + 2 * rank]
+        for k in range(points // step):
+            cols = pl.ds(k * step, step)
+            right = jnp.concatenate([spec_ref[:, cols], spec_ref[: 4 * nb, cols]], axis=0)
+            add = jnp.dot(lh, right, preferred_element_type=F32)
+            ob[h, cols] = (gh * ub[h, cols].astype(F32) + add).astype(BF)
+        stores[i].start()
     for store in stores:
         store.wait()
 
@@ -290,25 +296,26 @@
     vmem = pl.BlockSpec(memory_space=pltpu.VMEM)
     smem = pl.BlockSpec(memory_space=pltpu.SMEM)
     hbm = pl.BlockSpec(memory_space=pl.ANY)
-    spec, coef, gram = pl.pallas_call(
+    spec, coef, gram, flat = pl.pallas_call(
         functools.partial(exchange, groups, spread),
         out_shape=(
             jax.ShapeDtypeStruct((8 * nb, points), BF),
             jax.ShapeDtypeStruct((2 * nb, 128), F32),
             jax.ShapeDtypeStruct((nb // 2, rank, 128), F32),
+            jax.ShapeDtypeStruct((nb * rows, points), BF),
         ),
         in_specs=[pl.BlockSpec(memory_space=pltpu.HBM)] * 3,
-        out_specs=(vmem, vmem, vmem),
+        out_specs=(vmem, vmem, vmem, vmem),
         scratch_shapes=[
             pltpu.SMEM(bins.shape, jnp.int32),
             pltpu.VMEM((2, slice_len, points), F32),
-            pltpu.VMEM((nb * rows, points), BF),
             pltpu.VMEM((groups, 2, 2 * nb, points), F32),
             pltpu.VMEM((3, 2, 2 * nb, points), F32),
             pltpu.VMEM((2, 2 * nb, points), F32),
             pltpu.VMEM((spread, 2 * nb, 128), F32),
             pltpu.VMEM((spread, nb // 2, rank, 128), F32),
-            pltpu.SemaphoreType.DMA((6,)),
+            pltpu.SemaphoreType.DMA((2, CHUNKS)),
+            pltpu.SemaphoreType.DMA((2 * nb + 1,)),
             pltpu.SemaphoreType.DMA((CHUNKS, 2, 3)),
             pltpu.SemaphoreType.DMA((CHUNKS, 2, 3)),
             pltpu.SemaphoreType.DMA((spread,)),
@@ -326,17 +333,15 @@
             jax.ShapeDtypeStruct(old_basis.shape, BF),
             jax.ShapeDtypeStruct((nb, 2, rank, rank), F32),
         ),
-        in_specs=[smem, vmem, vmem, vmem, vmem, hbm],
+        in_specs=[smem, vmem, vmem, vmem, vmem, vmem],
         out_specs=(hbm, vmem),
         scratch_shapes=[
             pltpu.VMEM((nb * rows, points), BF),
-            pltpu.VMEM((nb * rows, points), BF),
-            pltpu.SemaphoreType.DMA((CHUNKS,)),
-            pltpu.SemaphoreType.DMA((CHUNKS,)),
+            pltpu.SemaphoreType.DMA((2 * nb,)),
         ],
         compiler_params=pltpu.CompilerParams(vmem_limit_bytes=40 * 2**20),
         name="update",
-    )(block_count, eigenvalues, coef, gram, spec, old_basis)
+    )(block_count, eigenvalues, coef, gram, spec, flat)
     return fresh, coherence
 
 

time: 32.5 us -> 26.9 us (0.83)
  Pallas kernels: 30.8 us -> 25.4 us
    pallas_call x1, Pallas kernels: 9.2 us -> 4.21 us  [local(): pl.pallas_call(update, out_shape=(jax.ShapeDtypeStruct(old_basis.shape, B...]
    pallas_call x1, Pallas kernels: 21.6 us -> 21.2 us  [local(): pl.pallas_call(functools.partial(exchange, groups, spread), out_shape=(ja...]
where the time goes in v3:
time: 26.9 us; the launch traced here: 26.7 us
  Pallas kernels  25.4 us (94%)
  between operations  1.31 us (5%)
    pallas_call x1, Pallas kernels, local(): pl.pallas_call(functools.partial(exchange, groups, spread), out_shape=(ja...  21.2 us
    pallas_call x1, Pallas kernels, local(): pl.pallas_call(update, out_shape=(jax.ShapeDtypeStruct(old_basis.shape, B...  4.21 us

profile of v3, /device:TPU:0, one launch (start us, length us, event | category | flops | bytes accessed | tf_op | source)
XLA Modules:
  0.0 26.7 jit_solution(4116107016089378269)
XLA Ops:
  0.6 0.0 copy-start
  1.3 21.2 %exchange.1 = (bf16[32,4096]{1,0:T(8,128)(2,1)S(1)}, f32[8,128]{1,0:T(8,128)S(1)}, f32[2,32,128]{2,1,0:T(8,128)S(1)}, bf16[512,4096]{1,0:T(8,128)(2,1)S(1)}) custom-call(s32[16]{0:T(128)} %bins_ref.1, f32[64,2,4096]{2,1,0:T(2,128)} %snap_ref.1, bf16[4,2,32,2,4096]{4,3,2,1,0:T(2,128)(2,1)} %basis_ref.1), custom_call_target="tpu_custom_call" | custom-call | tf_op jit(solution)/shard_map/exchange/pallas_call | solution.py:299
  22.5 0.0 copy-done
  22.5 4.2 %update.1 = (bf16[4,2,32,2,4096]{4,3,2,1,0:T(2,128)(2,1)}, f32[4,2,32,32]{3,2,1,0:T(8,128)}) custom-call(s32[1]{0:T(128)S(6)} %copy.7.count_ref, f32[4,32]{1,0:T(4,128)S(1)} %copy-done, f32[8,128]{1,0:T(8,128)S(1)} %get-tuple-element.6.coef_ref, f32[2,32,128]{2,1,0:T(8,128)S(1)} %get-tuple-element.7.gram_ref, ...), custom_call_target="tpu_custom_call" | custom-call | tf_op jit(solution)/shard_map/update/pallas_call | solution.py:330
Async XLA Ops:
  0.6 21.9 %copy-start = (f32[4,32]{1,0:T(4,128)S(1)}, f32[4,32]{1,0:T(4,128)}, u32[]{:S(2)}) copy-start(f32[4,32]{1,0:T(4,128)} %eig_ref.1) | copy-start | bytes 1540

commit v4 on v3

--- a/solution.py
+++ b/solution.py
@@ -56,7 +56,7 @@
 
 
 def exchange(groups, spread, bins_ref, snap_ref, basis_ref, spec_ref, coef_ref, gram_ref, ub,
-             bins, xs, terms, recv, fwd, cbuf, gbuf, in_sem, b_sem, rs_send, rs_recv, g_send, g_recv, c_send, c_recv):
+             bins, xs, terms, recv, fwd, cbuf, gsum, gbuf, in_sem, b_sem, rs_send, rs_recv, g_send, g_recv, h_send, h_recv, c_send, c_recv):
     assert groups == 4
     slice_len = snap_ref.shape[0]
     points = snap_ref.shape[2]
@@ -146,30 +146,58 @@
     pr, pc = iota((2 * two, 128), 0), iota((2 * two, 128), 1)
     place = ones_where(pc == mod(div(pr, 2), rank) + 2 * rank * mod(div(pr, rows), 2) + rank * div(pr, two))
     fold = ones_where(iota((rank, 3 * two), 0) == mod(div(iota((rank, 3 * two), 1), 2), rank))
+    late = CHUNKS // 2
+    for k in range(late):
+        pass_on(k)
     for p in range(nb // 2):
         for load in load_basis[4 * p:4 * p + 4]:
             load.wait()
         w = ub[pl.ds(p * two, two), :]
         big = dot_nt(w, w)
-        for k in range(p * CHUNKS // nb, (p + 1) * CHUNKS // nb):
+        for k in range(late + p * late // (nb // 2), late + (p + 1) * late // (nb // 2)):
             pass_on(k)
         wide = right_pick(jnp.concatenate([big * keep_re, big * keep_im], axis=1), place)
-        gbuf[me_s, p] = jnp.dot(fold, jnp.concatenate(split3(wide), axis=0), preferred_element_type=F32)
-    g_copies = []
-    for d in range(1, spread):
-        copy = pltpu.make_async_remote_copy(
-            src_ref=gbuf.at[me_s], dst_ref=gbuf.at[me_s], send_sem=g_send.at[d], recv_sem=g_recv.at[d],
-            device_id=(me_t, lax.rem(me_s + d, spread)), device_id_type=MESH)
-        copy.start()
-        g_copies.append(copy)
-    for k in range((nb // 2) * CHUNKS // nb, CHUNKS):
-        pass_on(k)
+        gsum[p * rank:(p + 1) * rank] = jnp.dot(
+            fold, jnp.concatenate(split3(wide), axis=0), preferred_element_type=F32)
+
+    def to_all(src, dst, send_sem, recv_sem):
+        out = []
+        for d in range(1, spread):
+            peer = lax.rem(me_s + d, spread)
+            out.append(pltpu.make_async_remote_copy(
+                src_ref=src(peer), dst_ref=dst, send_sem=send_sem.at[d], recv_sem=recv_sem.at[d],
+                device_id=(me_t, peer), device_id_type=MESH))
+            out[-1].start()
+        return out
+
+    g_rows = nb // 2 * rank
+    share = g_rows // spread if g_rows % (8 * spread) == 0 else g_rows
+    shared = share < g_rows
+
+    def mine(device):
+        return pl.ds(pl.multiple_of(device * share, 8), share) if shared else slice(None)
+
+    g_copies = to_all(lambda peer: gsum.at[mine(peer)], gbuf.at[me_s], g_send, g_recv)
+
+    def sum_gram():
+        for copy in g_copies:
+            copy.wait_recv()
+        gbuf[me_s] = gsum[mine(me_s)]
+        gram = gbuf[0]
+        for s in range(1, spread):
+            gram = gram + gbuf[s]
+        gram_ref[mine(me_s)] = gram
+        if not shared:
+            return []
+        return to_all(lambda peer: gram_ref.at[mine(me_s)], gram_ref.at[mine(me_s)], h_send, h_recv)
 
     er, ec = iota((nb * rows, 128), 0), iota((nb * rows, 128), 1)
     pick = ones_where(mod(div(er, 2), rank) == ec)
     acc = jnp.zeros((8 * nb, nb * rows), F32)
     square = jnp.zeros((2 * nb, 128), F32)
     for k in range(CHUNKS):
+        if k == CHUNKS - 1:
+            h_copies = sum_gram()
         cols = pl.ds(k * step, step)
         for v in range(2):
             copies[k, v, 1].wait_recv()
@@ -190,28 +218,16 @@
     coef = right_pick(jnp.where(div(ar, 2) == div(ac, rows), acc, 0.0), pick)
     norm = jnp.sum(square, axis=1, keepdims=True)
     cbuf[me_s] = jnp.where(iota((2 * nb, 128), 1) == rank, norm, coef)
-    c_copies = []
-    for d in range(1, spread):
-        copy = pltpu.make_async_remote_copy(
-            src_ref=cbuf.at[me_s], dst_ref=cbuf.at[me_s], send_sem=c_send.at[d], recv_sem=c_recv.at[d],
-            device_id=(me_t, lax.rem(me_s + d, spread)), device_id_type=MESH)
-        copy.start()
-        c_copies.append(copy)
-    for copy in g_copies:
-        copy.wait_recv()
-    gram = gbuf[0]
-    for s in range(1, spread):
-        gram = gram + gbuf[s]
-    gram_ref[...] = gram
+    c_copies = to_all(lambda peer: cbuf.at[me_s], cbuf.at[me_s], c_send, c_recv)
     for copy in list(copies.values()) + g_copies:
         copy.wait_send()
-    for copy in c_copies:
+    for copy in h_copies + c_copies:
         copy.wait_recv()
     coef = cbuf[0]
     for s in range(1, spread):
         coef = coef + cbuf[s]
     coef_ref[...] = coef
-    for copy in c_copies:
+    for copy in h_copies + c_copies:
         copy.wait_send()
 
 
@@ -222,11 +238,11 @@
     flat_out = fresh_ref.reshape(nb * rows, points)
     halves = [pl.ds(h * 2 * rank, 2 * rank) for h in range(2 * nb)]
     stores = [pltpu.make_async_copy(ob.at[h], flat_out.at[h], out_sem.at[i]) for i, h in enumerate(halves)]
-    count = jnp.full((1, 1), count_ref[0], jnp.int32).astype(F32)
+    coef = coef_ref[...]
+    count = count_ref[...].astype(F32)
     w_old = count / (count + 1.0)
     w_new = 1.0 / (count + 1.0)
     scaled = w_old * eig_ref[...]
-    coef = coef_ref[...]
     coef_t = jnp.transpose(coef)
     scaled_t = jnp.transpose(jnp.concatenate([scaled, scaled], axis=0))
     eye = iota((rank, rank), 0) == iota((rank, rank), 1)
@@ -236,7 +252,7 @@
     k_a = jnp.zeros((2 * nb, 128), F32)
     pad = jnp.zeros((1, 128 - rank), F32)
     for b in range(nb):
-        g = gram_ref[b // 2]
+        g = gram_ref[b // 2 * rank:(b // 2 + 1) * rank]
         at = 2 * rank * (b % 2)
         g_re, g_im = g[:, at:at + rank], g[:, at + rank:at + 2 * rank]
         cr, ci = coef[2 * b:2 * b + 1, :rank], coef[2 * b + 1:2 * b + 2, :rank]
@@ -293,15 +309,16 @@
     slice_len, _, points = snapshots.shape
     nb, _, rank = old_basis.shape[:3]
     rows = 4 * rank
+    g_rows = nb // 2 * rank
+    share = g_rows // spread if g_rows % (8 * spread) == 0 else g_rows
     vmem = pl.BlockSpec(memory_space=pltpu.VMEM)
-    smem = pl.BlockSpec(memory_space=pltpu.SMEM)
     hbm = pl.BlockSpec(memory_space=pl.ANY)
     spec, coef, gram, flat = pl.pallas_call(
         functools.partial(exchange, groups, spread),
         out_shape=(
             jax.ShapeDtypeStruct((8 * nb, points), BF),
             jax.ShapeDtypeStruct((2 * nb, 128), F32),
-            jax.ShapeDtypeStruct((nb // 2, rank, 128), F32),
+            jax.ShapeDtypeStruct((g_rows, 128), F32),
             jax.ShapeDtypeStruct((nb * rows, points), BF),
         ),
         in_specs=[pl.BlockSpec(memory_space=pltpu.HBM)] * 3,
@@ -313,11 +330,14 @@
             pltpu.VMEM((3, 2, 2 * nb, points), F32),
             pltpu.VMEM((2, 2 * nb, points), F32),
             pltpu.VMEM((spread, 2 * nb, 128), F32),
-            pltpu.VMEM((spread, nb // 2, rank, 128), F32),
+            pltpu.VMEM((g_rows, 128), F32),
+            pltpu.VMEM((spread, share, 128), F32),
             pltpu.SemaphoreType.DMA((2, CHUNKS)),
             pltpu.SemaphoreType.DMA((2 * nb + 1,)),
             pltpu.SemaphoreType.DMA((CHUNKS, 2, 3)),
             pltpu.SemaphoreType.DMA((CHUNKS, 2, 3)),
+            pltpu.SemaphoreType.DMA((spread,)),
+            pltpu.SemaphoreType.DMA((spread,)),
             pltpu.SemaphoreType.DMA((spread,)),
             pltpu.SemaphoreType.DMA((spread,)),
             pltpu.SemaphoreType.DMA((spread,)),
@@ -333,7 +353,7 @@
             jax.ShapeDtypeStruct(old_basis.shape, BF),
             jax.ShapeDtypeStruct((nb, 2, rank, rank), F32),
         ),
-        in_specs=[smem, vmem, vmem, vmem, vmem, vmem],
+        in_specs=[vmem, vmem, vmem, vmem, vmem, vmem],
         out_specs=(hbm, vmem),
         scratch_shapes=[
             pltpu.VMEM((nb * rows, points), BF),
@@ -341,7 +361,7 @@
         ],
         compiler_params=pltpu.CompilerParams(vmem_limit_bytes=40 * 2**20),
         name="update",
-    )(block_count, eigenvalues, coef, gram, spec, flat)
+    )(block_count.reshape(1, 1), eigenvalues, coef, gram, spec, flat)
     return fresh, coherence
 
 

time: 26.9 us -> 30.1 us (1.12)
  Pallas kernels: 25.4 us -> 28.6 us
    pallas_call x1, Pallas kernels: 21.2 us -> 24.2 us  [local(): pl.pallas_call(functools.partial(exchange, groups, spread), out_shape=(ja...]
where the time goes in v4:
time: 30.1 us; the launch traced here: 29.9 us
  Pallas kernels  28.6 us (95%)
  between operations  1.31 us (4%)
    pallas_call x1, Pallas kernels, local(): pl.pallas_call(functools.partial(exchange, groups, spread), out_shape=(ja...  24.2 us
    pallas_call x1, Pallas kernels, local(): pl.pallas_call(update, out_shape=(jax.ShapeDtypeStruct(old_basis.shape, B...  4.36 us

profile of v4, /device:TPU:0, one launch (start us, length us, event | category | flops | bytes accessed | tf_op | source)
XLA Modules:
  0.0 29.9 jit_solution(3784118701939002672)
XLA Ops:
  0.6 0.0 copy-start
  1.3 24.2 %exchange.1 = (bf16[32,4096]{1,0:T(8,128)(2,1)S(1)}, f32[8,128]{1,0:T(8,128)S(1)}, f32[64,128]{1,0:T(8,128)S(1)}, bf16[512,4096]{1,0:T(8,128)(2,1)S(1)}) custom-call(s32[16]{0:T(128)} %bins_ref.1, f32[64,2,4096]{2,1,0:T(2,128)} %snap_ref.1, bf16[4,2,32,2,4096]{4,3,2,1,0:T(2,128)(2,1)} %basis_ref.1), custom_call_target="tpu_custom_call" | custom-call | tf_op jit(solution)/shard_map/exchange/pallas_call | solution.py:316
  25.5 0.0 copy-done
  25.5 4.4 %update.1 = (bf16[4,2,32,2,4096]{4,3,2,1,0:T(2,128)(2,1)}, f32[4,2,32,32]{3,2,1,0:T(8,128)}) custom-call(s32[1,1]{1,0:T(1,128)} %bitcast.1.count_ref, f32[4,32]{1,0:T(4,128)S(1)} %copy-done, f32[8,128]{1,0:T(8,128)S(1)} %get-tuple-element.6.coef_ref, f32[64,128]{1,0:T(8,128)S(1)} %get-tuple-element.7.gram_ref, ...), custom_call_target="tpu_custom_call" | custom-call | tf_op jit(solution)/shard_map/update/pallas_call | solution.py:350
Async XLA Ops:
  0.6 24.9 %copy-start = (f32[4,32]{1,0:T(4,128)S(1)}, f32[4,32]{1,0:T(4,128)}, u32[]{:S(2)}) copy-start(f32[4,32]{1,0:T(4,128)} %eig_ref.1) | copy-start | bytes 1540

commit v5 on v4

--- a/solution.py
+++ b/solution.py
@@ -11,7 +11,7 @@
 MESH = pl.DeviceIdType.MESH
 BF = jnp.bfloat16
 F32 = jnp.float32
-CHUNKS = 8
+CHUNKS = 4
 LIMIT = 40 * 2**20
 
 
@@ -56,7 +56,7 @@
 
 
 def exchange(groups, spread, bins_ref, snap_ref, basis_ref, spec_ref, coef_ref, gram_ref, ub,
-             bins, xs, terms, recv, fwd, cbuf, gsum, gbuf, in_sem, b_sem, rs_send, rs_recv, g_send, g_recv, h_send, h_recv, c_send, c_recv):
+             bins, xs, terms, recv, fwd, cbuf, gsum, gbuf, in_sem, b_sem, rs_send, rs_recv, sa_sem):
     assert groups == 4
     slice_len = snap_ref.shape[0]
     points = snap_ref.shape[2]
@@ -67,75 +67,82 @@
     total = slice_len * groups
     me_t = lax.axis_index("ta")
     me_s = lax.axis_index("sa")
-    load_bins = pltpu.make_async_copy(bins_ref, bins, b_sem.at[2 * nb])
+    load_bins = pltpu.make_async_copy(bins_ref, bins, b_sem.at[nb // 2])
     load_bins.start()
     parts = [pl.ds(k * step, step) for k in range(CHUNKS)]
-    loads = [[pltpu.make_async_copy(snap_ref.at[:, v, p], xs.at[v, :, p], in_sem.at[v, k]) for v in range(2)]
-             for k, p in enumerate(parts)]
-    for pair in loads:
-        for load in pair:
-            load.start()
+    flat_snap = snap_ref.reshape(2 * slice_len, points)
+    loads = [pltpu.make_async_copy(flat_snap.at[:, p], xs.at[:, p], in_sem.at[k]) for k, p in enumerate(parts)]
+    for load in loads:
+        load.start()
     flat = basis_ref.reshape(nb * rows, points)
-    halves = [pl.ds(h * 2 * rank, 2 * rank) for h in range(2 * nb)]
-    load_basis = [pltpu.make_async_copy(flat.at[h], ub.at[h], b_sem.at[i]) for i, h in enumerate(halves)]
+    pairs = [pl.ds(p * 2 * rows, 2 * rows) for p in range(nb // 2)]
+    load_basis = [pltpu.make_async_copy(flat.at[h], ub.at[h], b_sem.at[i]) for i, h in enumerate(pairs)]
 
     near = me_t + 1 - 2 * lax.rem(me_t, 2)
     far = lax.rem(me_t + 2, 4)
-    diagonal = lax.rem(near + 2, 4)
     barrier = pltpu.get_barrier_semaphore()
     for peer in (near, far):
         pl.semaphore_signal(barrier, inc=1, device_id=(peer, me_s), device_id_type=MESH)
     for d in range(1, spread):
         pl.semaphore_signal(barrier, inc=1, device_id=(me_t, lax.rem(me_s + d, spread)), device_id_type=MESH)
 
-    t = iota((2 * nbins, slice_len), 1) + me_t * slice_len
-    row = iota((2 * nbins, slice_len), 0)
+    shape = (4 * nbins, 2 * slice_len)
+    row, col = iota(shape, 0), iota(shape, 1)
+    t = div(col, 2) + me_t * slice_len
     unit = 2.0 * math.pi / total
     window = (0.5 - 0.5 * jnp.cos(unit * t[:8].astype(F32))) * math.sqrt(8.0 / (3.0 * total))
-    window = jnp.concatenate([window] * (2 * nbins // 8), axis=0)
+    window = jnp.concatenate([window] * (4 * nbins // 8), axis=0)
+    slot = mod(div(row, 2 * nb), 4)
+    group = jnp.where(row < 2 * nbins, 2 * mod(slot, 2) + div(slot, 2), slot)
+    index = group * nb + div(mod(row, 2 * nb), 2)
     load_bins.wait()
-    bin_of = jnp.zeros((2 * nbins, slice_len), jnp.int32)
+    bin_of = jnp.zeros(shape, jnp.int32)
     for b in range(nbins):
-        bin_of = jnp.where(div(row, 2) == b, bins[b], bin_of)
+        bin_of = jnp.where(index == b, bins[b], bin_of)
     phase = jnp.bitwise_and(bin_of * t + mod(row, 2) * (total // 4), total - 1)
-    th, tl = split(jnp.cos(unit * phase.astype(F32)) * window)
+    table = jnp.cos(unit * phase.astype(F32)) * window
+    th, tl = split(jnp.where(div(row, 2 * nbins) == mod(col, 2), table, 0.0))
     left = jnp.concatenate(
         [jnp.concatenate([th, th], axis=1), jnp.concatenate([tl, jnp.zeros_like(tl)], axis=1)], axis=0)
 
     pl.semaphore_wait(barrier, 2 + spread - 1)
 
-    def rs_copy(src, slot, v, k, peer):
-        cols = pl.ds(k * step, step)
+    first, second = (near, far), (far, near)
+    low, high = lax.rem(me_t, 2), me_t // 2
+    out_pair = (2 * lax.rem(near, 2), 2 * (far // 2))
+    own_slot = (2 * low + high, me_t)
+    pass_slot = (2 * low + 1 - high, near)
+    own_at, pass_at = (high, low), (1 - high, 1 - low)
+
+    def step_one(v, cols, k):
         return pltpu.make_async_remote_copy(
-            src_ref=src.at[v, :, cols], dst_ref=recv.at[slot, v, :, cols],
-            send_sem=rs_send.at[k, v, slot], recv_sem=rs_recv.at[k, v, slot],
-            device_id=(peer, me_s), device_id_type=MESH)
-
-    first, second = (near, far), (far, near)
-    copies = {}
-    for k in range(CHUNKS):
+            src_ref=terms.at[v, pl.ds(out_pair[v], 2), :, cols], dst_ref=recv.at[v, pl.ds(0, 2), :, cols],
+            send_sem=rs_send.at[0, v], recv_sem=rs_recv.at[0, v, k],
+            device_id=(first[v], me_s), device_id_type=MESH)
+
+    def step_two(v, cols, k):
+        return pltpu.make_async_remote_copy(
+            src_ref=fwd.at[v, :, cols], dst_ref=recv.at[v, 2, :, cols],
+            send_sem=rs_send.at[1, v], recv_sem=rs_recv.at[1, v, k],
+            device_id=(second[v], me_s), device_id_type=MESH)
+
+    for k, cols in enumerate(parts):
+        loads[k].wait()
+        out = jnp.dot(left, jnp.concatenate(split(xs[:, cols]), axis=0), preferred_element_type=F32)
+        out = out[: 4 * nbins] + out[4 * nbins:]
+        terms[:, :, :, cols] = out.reshape(2, groups, 2 * nb, step)
+        for v in range(2):
+            step_one(v, cols, k).start()
+        if k == 0:
+            for load in load_basis:
+                load.start()
+
+    def pass_on(k):
         cols = parts[k]
         for v in range(2):
-            loads[k][v].wait()
-            xh, xl = split(xs[v, :, cols])
-            out = jnp.dot(left, jnp.concatenate([xh, xl], axis=0), preferred_element_type=F32)
-            out = out[: 2 * nbins] + out[2 * nbins:]
-            terms[:, v, :, cols] = out.reshape(groups, 2 * nb, step)
-            copies[k, v, 0] = rs_copy(terms.at[diagonal], 0, v, k, first[v])
-            copies[k, v, 1] = rs_copy(terms.at[first[v]], 1, v, k, first[v])
-            copies[k, v, 0].start()
-            copies[k, v, 1].start()
-        if k == 1:
-            for load in load_basis:
-                load.start()
-
-    def pass_on(k):
-        cols = pl.ds(k * step, step)
-        for v in range(2):
-            copies[k, v, 0].wait_recv()
-            fwd[v, :, cols] = terms[second[v], v, :, cols] + recv[0, v, :, cols]
-            copies[k, v, 2] = rs_copy(fwd, 2, v, k, second[v])
-            copies[k, v, 2].start()
+            step_one(v, cols, k).wait_recv()
+            fwd[v, :, cols] = terms[v, pass_slot[v], :, cols] + recv[v, pass_at[v], :, cols]
+            step_two(v, cols, k).start()
 
     two = 2 * rows
     ri, ci = iota((two, two), 0), iota((two, two), 1)
@@ -146,29 +153,27 @@
     pr, pc = iota((2 * two, 128), 0), iota((2 * two, 128), 1)
     place = ones_where(pc == mod(div(pr, 2), rank) + 2 * rank * mod(div(pr, rows), 2) + rank * div(pr, two))
     fold = ones_where(iota((rank, 3 * two), 0) == mod(div(iota((rank, 3 * two), 1), 2), rank))
-    late = CHUNKS // 2
-    for k in range(late):
-        pass_on(k)
+    bigs = []
     for p in range(nb // 2):
-        for load in load_basis[4 * p:4 * p + 4]:
-            load.wait()
+        load_basis[p].wait()
         w = ub[pl.ds(p * two, two), :]
-        big = dot_nt(w, w)
-        for k in range(late + p * late // (nb // 2), late + (p + 1) * late // (nb // 2)):
+        bigs.append(dot_nt(w, w))
+        for k in range(p * CHUNKS // (nb // 2), (p + 1) * CHUNKS // (nb // 2)):
             pass_on(k)
+    for p, big in enumerate(bigs):
         wide = right_pick(jnp.concatenate([big * keep_re, big * keep_im], axis=1), place)
         gsum[p * rank:(p + 1) * rank] = jnp.dot(
             fold, jnp.concatenate(split3(wide), axis=0), preferred_element_type=F32)
 
     def to_all(src, dst, send_sem, recv_sem):
-        out = []
         for d in range(1, spread):
             peer = lax.rem(me_s + d, spread)
-            out.append(pltpu.make_async_remote_copy(
-                src_ref=src(peer), dst_ref=dst, send_sem=send_sem.at[d], recv_sem=recv_sem.at[d],
-                device_id=(me_t, peer), device_id_type=MESH))
-            out[-1].start()
-        return out
+            pltpu.make_async_remote_copy(
+                src_ref=src(peer), dst_ref=dst, send_sem=send_sem, recv_sem=recv_sem,
+                device_id=(me_t, peer), device_id_type=MESH).start()
+
+    def wait_all(like, sem):
+        pltpu.make_async_copy(like, like, sem).wait()
 
     g_rows = nb // 2 * rank
     share = g_rows // spread if g_rows % (8 * spread) == 0 else g_rows
@@ -177,32 +182,30 @@
     def mine(device):
         return pl.ds(pl.multiple_of(device * share, 8), share) if shared else slice(None)
 
-    g_copies = to_all(lambda peer: gsum.at[mine(peer)], gbuf.at[me_s], g_send, g_recv)
+    others = pl.ds(0, spread - 1)
+    to_all(lambda peer: gsum.at[mine(peer)], gbuf.at[me_s], sa_sem.at[0], sa_sem.at[1])
 
     def sum_gram():
-        for copy in g_copies:
-            copy.wait_recv()
+        wait_all(gbuf.at[others], sa_sem.at[1])
         gbuf[me_s] = gsum[mine(me_s)]
         gram = gbuf[0]
         for s in range(1, spread):
             gram = gram + gbuf[s]
         gram_ref[mine(me_s)] = gram
-        if not shared:
-            return []
-        return to_all(lambda peer: gram_ref.at[mine(me_s)], gram_ref.at[mine(me_s)], h_send, h_recv)
+        if shared:
+            to_all(lambda peer: gram_ref.at[mine(me_s)], gram_ref.at[mine(me_s)], sa_sem.at[2], sa_sem.at[3])
 
     er, ec = iota((nb * rows, 128), 0), iota((nb * rows, 128), 1)
     pick = ones_where(mod(div(er, 2), rank) == ec)
     acc = jnp.zeros((8 * nb, nb * rows), F32)
     square = jnp.zeros((2 * nb, 128), F32)
-    for k in range(CHUNKS):
+    for k, cols in enumerate(parts):
         if k == CHUNKS - 1:
-            h_copies = sum_gram()
-        cols = pl.ds(k * step, step)
+            sum_gram()
         for v in range(2):
-            copies[k, v, 1].wait_recv()
-            copies[k, v, 2].wait_recv()
-        spec = terms[me_t, :, :, cols] + recv[1, :, :, cols] + recv[2, :, :, cols]
+            step_two(v, cols, k).wait_recv()
+        spec = jnp.stack([terms[v, own_slot[v], :, cols] + recv[v, own_at[v], :, cols] + recv[v, 2, :, cols]
+                          for v in range(2)])
         sq = spec[0] * spec[0] + spec[1] * spec[1]
         for i in range(step // 128):
             square = square + sq[:, i * 128:(i + 1) * 128]
@@ -218,17 +221,21 @@
     coef = right_pick(jnp.where(div(ar, 2) == div(ac, rows), acc, 0.0), pick)
     norm = jnp.sum(square, axis=1, keepdims=True)
     cbuf[me_s] = jnp.where(iota((2 * nb, 128), 1) == rank, norm, coef)
-    c_copies = to_all(lambda peer: cbuf.at[me_s], cbuf.at[me_s], c_send, c_recv)
-    for copy in list(copies.values()) + g_copies:
-        copy.wait_send()
-    for copy in h_copies + c_copies:
-        copy.wait_recv()
+    to_all(lambda peer: cbuf.at[me_s], cbuf.at[me_s], sa_sem.at[4], sa_sem.at[5])
+    every = pl.ds(0, points)
+    for v in range(2):
+        step_one(v, every, 0).wait_send()
+        step_two(v, every, 0).wait_send()
+    wait_all(gbuf.at[others], sa_sem.at[0])
+    if shared:
+        wait_all(gbuf.at[others], sa_sem.at[2])
+        wait_all(gbuf.at[others], sa_sem.at[3])
+    wait_all(cbuf.at[others], sa_sem.at[4])
+    wait_all(cbuf.at[others], sa_sem.at[5])
     coef = cbuf[0]
     for s in range(1, spread):
         coef = coef + cbuf[s]
     coef_ref[...] = coef
-    for copy in h_copies + c_copies:
-        copy.wait_send()
 
 
 def update(count_ref, eig_ref, coef_ref, gram_ref, spec_ref, ub, fresh_ref, coh_ref, ob, out_sem):
@@ -325,23 +332,18 @@
         out_specs=(vmem, vmem, vmem, vmem),
         scratch_shapes=[
             pltpu.SMEM(bins.shape, jnp.int32),
-            pltpu.VMEM((2, slice_len, points), F32),
-            pltpu.VMEM((groups, 2, 2 * nb, points), F32),
-            pltpu.VMEM((3, 2, 2 * nb, points), F32),
+            pltpu.VMEM((2 * slice_len, points), F32),
+            pltpu.VMEM((2, groups, 2 * nb, points), F32),
+            pltpu.VMEM((2, 3, 2 * nb, points), F32),
             pltpu.VMEM((2, 2 * nb, points), F32),
             pltpu.VMEM((spread, 2 * nb, 128), F32),
             pltpu.VMEM((g_rows, 128), F32),
             pltpu.VMEM((spread, share, 128), F32),
-            pltpu.SemaphoreType.DMA((2, CHUNKS)),
-            pltpu.SemaphoreType.DMA((2 * nb + 1,)),
-            pltpu.SemaphoreType.DMA((CHUNKS, 2, 3)),
-            pltpu.SemaphoreType.DMA((CHUNKS, 2, 3)),
-            pltpu.SemaphoreType.DMA((spread,)),
-            pltpu.SemaphoreType.DMA((spread,)),
-            pltpu.SemaphoreType.DMA((spread,)),
-            pltpu.SemaphoreType.DMA((spread,)),
-            pltpu.SemaphoreType.DMA((spread,)),
-            pltpu.SemaphoreType.DMA((spread,)),
+            pltpu.SemaphoreType.DMA((CHUNKS,)),
+            pltpu.SemaphoreType.DMA((nb // 2 + 1,)),
+            pltpu.SemaphoreType.DMA((2, 2)),
+            pltpu.SemaphoreType.DMA((2, 2, CHUNKS)),
+            pltpu.SemaphoreType.DMA((6,)),
         ],
         compiler_params=pltpu.CompilerParams(
             collective_id=0, has_side_effects=True, vmem_limit_bytes=LIMIT),

time: 30.1 us -> 29.1 us (0.967)
  Pallas kernels: 28.6 us -> 27.6 us
    pallas_call x1, Pallas kernels: 24.2 us -> 23.3 us  [local(): pl.pallas_call(functools.partial(exchange, groups, spread), out_shape=(ja...]
where the time goes in v5:
time: 29.1 us; the launch traced here: 29 us
  Pallas kernels  27.6 us (95%)
  between operations  1.31 us (5%)
    pallas_call x1, Pallas kernels, local(): pl.pallas_call(functools.partial(exchange, groups, spread), out_shape=(ja...  23.3 us
    pallas_call x1, Pallas kernels, local(): pl.pallas_call(update, out_shape=(jax.ShapeDtypeStruct(old_basis.shape, B...  4.33 us

profile of v5, /device:TPU:0, one launch (start us, length us, event | category | flops | bytes accessed | tf_op | source)
XLA Modules:
  0.0 29.0 jit_solution(7870718004771828325)
XLA Ops:
  0.6 0.0 copy-start
  1.3 23.3 %exchange.1 = (bf16[32,4096]{1,0:T(8,128)(2,1)S(1)}, f32[8,128]{1,0:T(8,128)S(1)}, f32[64,128]{1,0:T(8,128)S(1)}, bf16[512,4096]{1,0:T(8,128)(2,1)S(1)}) custom-call(s32[16]{0:T(128)} %bins_ref.1, f32[64,2,4096]{2,1,0:T(2,128)} %snap_ref.1, bf16[4,2,32,2,4096]{4,3,2,1,0:T(2,128)(2,1)} %basis_ref.1), custom_call_target="tpu_custom_call" | custom-call | tf_op jit(solution)/shard_map/exchange/pallas_call | solution.py:323
  24.6 0.0 copy-done
  24.6 4.3 %update.1 = (bf16[4,2,32,2,4096]{4,3,2,1,0:T(2,128)(2,1)}, f32[4,2,32,32]{3,2,1,0:T(8,128)}) custom-call(s32[1,1]{1,0:T(1,128)} %bitcast.1.count_ref, f32[4,32]{1,0:T(4,128)S(1)} %copy-done, f32[8,128]{1,0:T(8,128)S(1)} %get-tuple-element.6.coef_ref, f32[64,128]{1,0:T(8,128)S(1)} %get-tuple-element.7.gram_ref, ...), custom_call_target="tpu_custom_call" | custom-call | tf_op jit(solution)/shard_map/update/pallas_call | solution.py:352
Async XLA Ops:
  0.6 24.0 %copy-start = (f32[4,32]{1,0:T(4,128)S(1)}, f32[4,32]{1,0:T(4,128)}, u32[]{:S(2)}) copy-start(f32[4,32]{1,0:T(4,128)} %eig_ref.1) | copy-start | bytes 1540

commit v6 on v5

--- a/solution.py
+++ b/solution.py
@@ -56,7 +56,7 @@
 
 
 def exchange(groups, spread, bins_ref, snap_ref, basis_ref, spec_ref, coef_ref, gram_ref, ub,
-             bins, xs, terms, recv, fwd, cbuf, gsum, gbuf, in_sem, b_sem, rs_send, rs_recv, sa_sem):
+             bins, xs, terms, recv, fwd, cbuf, gbuf, in_sem, b_sem, rs_send, rs_recv, sa_sem):
     assert groups == 4
     slice_len = snap_ref.shape[0]
     points = snap_ref.shape[2]
@@ -160,10 +160,14 @@
         bigs.append(dot_nt(w, w))
         for k in range(p * CHUNKS // (nb // 2), (p + 1) * CHUNKS // (nb // 2)):
             pass_on(k)
-    for p, big in enumerate(bigs):
+    lane = iota((rank, 128), 1)
+    upper = mod(lane, rank) >= iota((rank, 128), 0)
+    packs = []
+    for big in bigs:
         wide = right_pick(jnp.concatenate([big * keep_re, big * keep_im], axis=1), place)
-        gsum[p * rank:(p + 1) * rank] = jnp.dot(
-            fold, jnp.concatenate(split3(wide), axis=0), preferred_element_type=F32)
+        both = jnp.dot(fold, jnp.concatenate(split3(wide), axis=0), preferred_element_type=F32)
+        packs.append(jnp.where(upper, both, pltpu.roll(both, 128 - rank, 1)))
+    gbuf[me_s] = jnp.where(mod(lane, 2 * rank) < rank, packs[0], pltpu.roll(packs[1], rank, 1))
 
     def to_all(src, dst, send_sem, recv_sem):
         for d in range(1, spread):
@@ -175,33 +179,14 @@
     def wait_all(like, sem):
         pltpu.make_async_copy(like, like, sem).wait()
 
-    g_rows = nb // 2 * rank
-    share = g_rows // spread if g_rows % (8 * spread) == 0 else g_rows
-    shared = share < g_rows
-
-    def mine(device):
-        return pl.ds(pl.multiple_of(device * share, 8), share) if shared else slice(None)
-
     others = pl.ds(0, spread - 1)
-    to_all(lambda peer: gsum.at[mine(peer)], gbuf.at[me_s], sa_sem.at[0], sa_sem.at[1])
-
-    def sum_gram():
-        wait_all(gbuf.at[others], sa_sem.at[1])
-        gbuf[me_s] = gsum[mine(me_s)]
-        gram = gbuf[0]
-        for s in range(1, spread):
-            gram = gram + gbuf[s]
-        gram_ref[mine(me_s)] = gram
-        if shared:
-            to_all(lambda peer: gram_ref.at[mine(me_s)], gram_ref.at[mine(me_s)], sa_sem.at[2], sa_sem.at[3])
+    to_all(lambda peer: gbuf.at[me_s], gbuf.at[me_s], sa_sem.at[0], sa_sem.at[1])
 
     er, ec = iota((nb * rows, 128), 0), iota((nb * rows, 128), 1)
     pick = ones_where(mod(div(er, 2), rank) == ec)
     acc = jnp.zeros((8 * nb, nb * rows), F32)
     square = jnp.zeros((2 * nb, 128), F32)
     for k, cols in enumerate(parts):
-        if k == CHUNKS - 1:
-            sum_gram()
         for v in range(2):
             step_two(v, cols, k).wait_recv()
         spec = jnp.stack([terms[v, own_slot[v], :, cols] + recv[v, own_at[v], :, cols] + recv[v, 2, :, cols]
@@ -221,17 +206,19 @@
     coef = right_pick(jnp.where(div(ar, 2) == div(ac, rows), acc, 0.0), pick)
     norm = jnp.sum(square, axis=1, keepdims=True)
     cbuf[me_s] = jnp.where(iota((2 * nb, 128), 1) == rank, norm, coef)
-    to_all(lambda peer: cbuf.at[me_s], cbuf.at[me_s], sa_sem.at[4], sa_sem.at[5])
+    to_all(lambda peer: cbuf.at[me_s], cbuf.at[me_s], sa_sem.at[2], sa_sem.at[3])
     every = pl.ds(0, points)
     for v in range(2):
         step_one(v, every, 0).wait_send()
         step_two(v, every, 0).wait_send()
     wait_all(gbuf.at[others], sa_sem.at[0])
-    if shared:
-        wait_all(gbuf.at[others], sa_sem.at[2])
-        wait_all(gbuf.at[others], sa_sem.at[3])
-    wait_all(cbuf.at[others], sa_sem.at[4])
-    wait_all(cbuf.at[others], sa_sem.at[5])
+    wait_all(gbuf.at[others], sa_sem.at[1])
+    gram = gbuf[0]
+    for s in range(1, spread):
+        gram = gram + gbuf[s]
+    gram_ref[...] = gram
+    wait_all(cbuf.at[others], sa_sem.at[2])
+    wait_all(cbuf.at[others], sa_sem.at[3])
     coef = cbuf[0]
     for s in range(1, spread):
         coef = coef + cbuf[s]
@@ -253,15 +240,20 @@
     coef_t = jnp.transpose(coef)
     scaled_t = jnp.transpose(jnp.concatenate([scaled, scaled], axis=0))
     eye = iota((rank, rank), 0) == iota((rank, rank), 1)
+    upper = iota((rank, rank), 0) <= iota((rank, rank), 1)
+    lower = iota((rank, rank), 0) > iota((rank, rank), 1)
+    gram = gram_ref[...]
+    gram_t = jnp.transpose(gram)
     r8 = iota((2 * nb, 128), 0)
     k_p = jnp.zeros((2 * nb, 128), F32)
     k_s = jnp.zeros((2 * nb, 128), F32)
     k_a = jnp.zeros((2 * nb, 128), F32)
     pad = jnp.zeros((1, 128 - rank), F32)
     for b in range(nb):
-        g = gram_ref[b // 2 * rank:(b // 2 + 1) * rank]
-        at = 2 * rank * (b % 2)
-        g_re, g_im = g[:, at:at + rank], g[:, at + rank:at + 2 * rank]
+        at = 2 * rank * (b % 2) + rank * (b // 2)
+        g, g_t = gram[:, at:at + rank], gram_t[at:at + rank]
+        g_re = jnp.where(upper, g, g_t)
+        g_im = jnp.where(lower, g, jnp.where(eye, 0.0, -g_t))
         cr, ci = coef[2 * b:2 * b + 1, :rank], coef[2 * b + 1:2 * b + 2, :rank]
         cr_c, ci_c = coef_t[:rank, 2 * b:2 * b + 1], coef_t[:rank, 2 * b + 1:2 * b + 2]
         norm = coef[2 * b:2 * b + 1, rank:rank + 1] + coef[2 * b + 1:2 * b + 2, rank:rank + 1]
@@ -316,8 +308,7 @@
     slice_len, _, points = snapshots.shape
     nb, _, rank = old_basis.shape[:3]
     rows = 4 * rank
-    g_rows = nb // 2 * rank
-    share = g_rows // spread if g_rows % (8 * spread) == 0 else g_rows
+    assert nb * rank == 128
     vmem = pl.BlockSpec(memory_space=pltpu.VMEM)
     hbm = pl.BlockSpec(memory_space=pl.ANY)
     spec, coef, gram, flat = pl.pallas_call(
@@ -325,7 +316,7 @@
         out_shape=(
             jax.ShapeDtypeStruct((8 * nb, points), BF),
             jax.ShapeDtypeStruct((2 * nb, 128), F32),
-            jax.ShapeDtypeStruct((g_rows, 128), F32),
+            jax.ShapeDtypeStruct((rank, 128), F32),
             jax.ShapeDtypeStruct((nb * rows, points), BF),
         ),
         in_specs=[pl.BlockSpec(memory_space=pltpu.HBM)] * 3,
@@ -337,13 +328,12 @@
             pltpu.VMEM((2, 3, 2 * nb, points), F32),
             pltpu.VMEM((2, 2 * nb, points), F32),
             pltpu.VMEM((spread, 2 * nb, 128), F32),
-            pltpu.VMEM((g_rows, 128), F32),
-            pltpu.VMEM((spread, share, 128), F32),
+            pltpu.VMEM((spread, rank, 128), F32),
             pltpu.SemaphoreType.DMA((CHUNKS,)),
             pltpu.SemaphoreType.DMA((nb // 2 + 1,)),
             pltpu.SemaphoreType.DMA((2, 2)),
             pltpu.SemaphoreType.DMA((2, 2, CHUNKS)),
-            pltpu.SemaphoreType.DMA((6,)),
+            pltpu.SemaphoreType.DMA((4,)),
         ],
         compiler_params=pltpu.CompilerParams(
             collective_id=0, has_side_effects=True, vmem_limit_bytes=LIMIT),

time: 29.1 us -> 28 us (0.962)
  Pallas kernels: 27.6 us -> 26.5 us
    pallas_call x1, Pallas kernels: 23.3 us -> 22.1 us  [local(): pl.pallas_call(functools.partial(exchange, groups, spread), out_shape=(ja...]
where the time goes in v6:
time: 28 us; the launch traced here: 27.8 us
  Pallas kernels  26.5 us (95%)
  between operations  1.31 us (5%)
    pallas_call x1, Pallas kernels, local(): pl.pallas_call(functools.partial(exchange, groups, spread), out_shape=(ja...  22.1 us
    pallas_call x1, Pallas kernels, local(): pl.pallas_call(update, out_shape=(jax.ShapeDtypeStruct(old_basis.shape, B...  4.41 us

profile of v6, /device:TPU:0, one launch (start us, length us, event | category | flops | bytes accessed | tf_op | source)
XLA Modules:
  0.0 27.8 jit_solution(13322092473147065964)
XLA Ops:
  0.6 0.0 copy-start
  1.3 22.1 %exchange.1 = (bf16[32,4096]{1,0:T(8,128)(2,1)S(1)}, f32[8,128]{1,0:T(8,128)S(1)}, f32[32,128]{1,0:T(8,128)S(1)}, bf16[512,4096]{1,0:T(8,128)(2,1)S(1)}) custom-call(s32[16]{0:T(128)} %bins_ref.1, f32[64,2,4096]{2,1,0:T(2,128)} %snap_ref.1, bf16[4,2,32,2,4096]{4,3,2,1,0:T(2,128)(2,1)} %basis_ref.1), custom_call_target="tpu_custom_call" | custom-call | tf_op jit(solution)/shard_map/exchange/pallas_call | solution.py:314
  23.4 0.0 copy-done
  23.4 4.4 %update.1 = (bf16[4,2,32,2,4096]{4,3,2,1,0:T(2,128)(2,1)}, f32[4,2,32,32]{3,2,1,0:T(8,128)}) custom-call(s32[1,1]{1,0:T(1,128)} %bitcast.1.count_ref, f32[4,32]{1,0:T(4,128)S(1)} %copy-done, f32[8,128]{1,0:T(8,128)S(1)} %get-tuple-element.6.coef_ref, f32[32,128]{1,0:T(8,128)S(1)} %get-tuple-element.7.gram_ref, ...), custom_call_target="tpu_custom_call" | custom-call | tf_op jit(solution)/shard_map/update/pallas_call | solution.py:342
Async XLA Ops:
  0.6 22.8 %copy-start = (f32[4,32]{1,0:T(4,128)S(1)}, f32[4,32]{1,0:T(4,128)}, u32[]{:S(2)}) copy-start(f32[4,32]{1,0:T(4,128)} %eig_ref.1) | copy-start | bytes 1540

commit v7 on v6

--- a/solution.py
+++ b/solution.py
@@ -11,7 +11,7 @@
 MESH = pl.DeviceIdType.MESH
 BF = jnp.bfloat16
 F32 = jnp.float32
-CHUNKS = 4
+CHUNKS = 8
 LIMIT = 40 * 2**20
 
 

time: 28 us -> 27.6 us (0.986)
  Pallas kernels: 26.5 us -> 26.1 us
    pallas_call x1, Pallas kernels: 22.1 us -> 21.7 us  [local(): pl.pallas_call(functools.partial(exchange, groups, spread), out_shape=(ja...]
where the time goes in v7:
time: 27.6 us; the launch traced here: 27.5 us
  Pallas kernels  26.1 us (95%)
  between operations  1.31 us (5%)
    pallas_call x1, Pallas kernels, local(): pl.pallas_call(functools.partial(exchange, groups, spread), out_shape=(ja...  21.7 us
    pallas_call x1, Pallas kernels, local(): pl.pallas_call(update, out_shape=(jax.ShapeDtypeStruct(old_basis.shape, B...  4.41 us

profile of v7, /device:TPU:0, one launch (start us, length us, event | category | flops | bytes accessed | tf_op | source)
XLA Modules:
  0.0 27.5 jit_solution(15170949466759805970)
XLA Ops:
  0.6 0.0 copy-start
  1.3 21.7 %exchange.1 = (bf16[32,4096]{1,0:T(8,128)(2,1)S(1)}, f32[8,128]{1,0:T(8,128)S(1)}, f32[32,128]{1,0:T(8,128)S(1)}, bf16[512,4096]{1,0:T(8,128)(2,1)S(1)}) custom-call(s32[16]{0:T(128)} %bins_ref.1, f32[64,2,4096]{2,1,0:T(2,128)} %snap_ref.1, bf16[4,2,32,2,4096]{4,3,2,1,0:T(2,128)(2,1)} %basis_ref.1), custom_call_target="tpu_custom_call" | custom-call | tf_op jit(solution)/shard_map/exchange/pallas_call | solution.py:314
  23.0 0.0 copy-done
  23.1 4.4 %update.1 = (bf16[4,2,32,2,4096]{4,3,2,1,0:T(2,128)(2,1)}, f32[4,2,32,32]{3,2,1,0:T(8,128)}) custom-call(s32[1,1]{1,0:T(1,128)} %bitcast.1.count_ref, f32[4,32]{1,0:T(4,128)S(1)} %copy-done, f32[8,128]{1,0:T(8,128)S(1)} %get-tuple-element.6.coef_ref, f32[32,128]{1,0:T(8,128)S(1)} %get-tuple-element.7.gram_ref, ...), custom_call_target="tpu_custom_call" | custom-call | tf_op jit(solution)/shard_map/update/pallas_call | solution.py:342
Async XLA Ops:
  0.6 22.4 %copy-start = (f32[4,32]{1,0:T(4,128)S(1)}, f32[4,32]{1,0:T(4,128)}, u32[]{:S(2)}) copy-start(f32[4,32]{1,0:T(4,128)} %eig_ref.1) | copy-start | bytes 1540

commit v8 on v3

--- a/solution.py
+++ b/solution.py
@@ -56,7 +56,7 @@
 
 
 def exchange(groups, spread, bins_ref, snap_ref, basis_ref, spec_ref, coef_ref, gram_ref, ub,
-             bins, xs, terms, recv, fwd, cbuf, gbuf, in_sem, b_sem, rs_send, rs_recv, g_send, g_recv, c_send, c_recv):
+             bins, xs, terms, recv, cbuf, gbuf, in_sem, b_sem, rs_send, rs_recv, g_send, g_recv, c_send, c_recv):
     assert groups == 4
     slice_len = snap_ref.shape[0]
     points = snap_ref.shape[2]
@@ -83,7 +83,7 @@
     far = lax.rem(me_t + 2, 4)
     diagonal = lax.rem(near + 2, 4)
     barrier = pltpu.get_barrier_semaphore()
-    for peer in (near, far):
+    for peer in (near, far, diagonal):
         pl.semaphore_signal(barrier, inc=1, device_id=(peer, me_s), device_id_type=MESH)
     for d in range(1, spread):
         pl.semaphore_signal(barrier, inc=1, device_id=(me_t, lax.rem(me_s + d, spread)), device_id_type=MESH)
@@ -102,16 +102,15 @@
     left = jnp.concatenate(
         [jnp.concatenate([th, th], axis=1), jnp.concatenate([tl, jnp.zeros_like(tl)], axis=1)], axis=0)
 
-    pl.semaphore_wait(barrier, 2 + spread - 1)
-
-    def rs_copy(src, slot, v, k, peer):
+    pl.semaphore_wait(barrier, 3 + spread - 1)
+
+    def rs_copy(slot, k, peer):
         cols = pl.ds(k * step, step)
         return pltpu.make_async_remote_copy(
-            src_ref=src.at[v, :, cols], dst_ref=recv.at[slot, v, :, cols],
-            send_sem=rs_send.at[k, v, slot], recv_sem=rs_recv.at[k, v, slot],
+            src_ref=terms.at[peer, :, :, cols], dst_ref=recv.at[slot, :, :, cols],
+            send_sem=rs_send.at[k, slot], recv_sem=rs_recv.at[k, slot],
             device_id=(peer, me_s), device_id_type=MESH)
 
-    first, second = (near, far), (far, near)
     copies = {}
     for k in range(CHUNKS):
         cols = parts[k]
@@ -121,21 +120,12 @@
             out = jnp.dot(left, jnp.concatenate([xh, xl], axis=0), preferred_element_type=F32)
             out = out[: 2 * nbins] + out[2 * nbins:]
             terms[:, v, :, cols] = out.reshape(groups, 2 * nb, step)
-            copies[k, v, 0] = rs_copy(terms.at[diagonal], 0, v, k, first[v])
-            copies[k, v, 1] = rs_copy(terms.at[first[v]], 1, v, k, first[v])
-            copies[k, v, 0].start()
-            copies[k, v, 1].start()
+        for slot, peer in enumerate((diagonal, near, far)):
+            copies[k, slot] = rs_copy(slot, k, peer)
+            copies[k, slot].start()
         if k == 1:
             for load in load_basis:
                 load.start()
-
-    def pass_on(k):
-        cols = pl.ds(k * step, step)
-        for v in range(2):
-            copies[k, v, 0].wait_recv()
-            fwd[v, :, cols] = terms[second[v], v, :, cols] + recv[0, v, :, cols]
-            copies[k, v, 2] = rs_copy(fwd, 2, v, k, second[v])
-            copies[k, v, 2].start()
 
     two = 2 * rows
     ri, ci = iota((two, two), 0), iota((two, two), 1)
@@ -151,8 +141,6 @@
             load.wait()
         w = ub[pl.ds(p * two, two), :]
         big = dot_nt(w, w)
-        for k in range(p * CHUNKS // nb, (p + 1) * CHUNKS // nb):
-            pass_on(k)
         wide = right_pick(jnp.concatenate([big * keep_re, big * keep_im], axis=1), place)
         gbuf[me_s, p] = jnp.dot(fold, jnp.concatenate(split3(wide), axis=0), preferred_element_type=F32)
     g_copies = []
@@ -162,8 +150,6 @@
             device_id=(me_t, lax.rem(me_s + d, spread)), device_id_type=MESH)
         copy.start()
         g_copies.append(copy)
-    for k in range((nb // 2) * CHUNKS // nb, CHUNKS):
-        pass_on(k)
 
     er, ec = iota((nb * rows, 128), 0), iota((nb * rows, 128), 1)
     pick = ones_where(mod(div(er, 2), rank) == ec)
@@ -171,10 +157,9 @@
     square = jnp.zeros((2 * nb, 128), F32)
     for k in range(CHUNKS):
         cols = pl.ds(k * step, step)
-        for v in range(2):
-            copies[k, v, 1].wait_recv()
-            copies[k, v, 2].wait_recv()
-        spec = terms[me_t, :, :, cols] + recv[1, :, :, cols] + recv[2, :, :, cols]
+        for slot in range(3):
+            copies[k, slot].wait_recv()
+        spec = (terms[me_t, :, :, cols] + recv[0, :, :, cols]) + (recv[1, :, :, cols] + recv[2, :, :, cols])
         sq = spec[0] * spec[0] + spec[1] * spec[1]
         for i in range(step // 128):
             square = square + sq[:, i * 128:(i + 1) * 128]
@@ -311,13 +296,12 @@
             pltpu.VMEM((2, slice_len, points), F32),
             pltpu.VMEM((groups, 2, 2 * nb, points), F32),
             pltpu.VMEM((3, 2, 2 * nb, points), F32),
-            pltpu.VMEM((2, 2 * nb, points), F32),
             pltpu.VMEM((spread, 2 * nb, 128), F32),
             pltpu.VMEM((spread, nb // 2, rank, 128), F32),
             pltpu.SemaphoreType.DMA((2, CHUNKS)),
             pltpu.SemaphoreType.DMA((2 * nb + 1,)),
-            pltpu.SemaphoreType.DMA((CHUNKS, 2, 3)),
-            pltpu.SemaphoreType.DMA((CHUNKS, 2, 3)),
+            pltpu.SemaphoreType.DMA((CHUNKS, 3)),
+            pltpu.SemaphoreType.DMA((CHUNKS, 3)),
             pltpu.SemaphoreType.DMA((spread,)),
             pltpu.SemaphoreType.DMA((spread,)),
             pltpu.SemaphoreType.DMA((spread,)),

time: 26.9 us -> 29.3 us (1.089)
  Pallas kernels: 25.4 us -> 27.8 us
    pallas_call x1, Pallas kernels: 21.2 us -> 23.5 us  [local(): pl.pallas_call(functools.partial(exchange, groups, spread), out_shape=(ja...]
where the time goes in v8:
time: 29.3 us; the launch traced here: 29.1 us
  Pallas kernels  27.8 us (95%)
  between operations  1.31 us (4%)
    pallas_call x1, Pallas kernels, local(): pl.pallas_call(functools.partial(exchange, groups, spread), out_shape=(ja...  23.5 us
    pallas_call x1, Pallas kernels, local(): pl.pallas_call(update, out_shape=(jax.ShapeDtypeStruct(old_basis.shape, B...  4.27 us

profile of v8, /device:TPU:0, one launch (start us, length us, event | category | flops | bytes accessed | tf_op | source)
XLA Modules:
  0.0 29.1 jit_solution(4422447870201839472)
XLA Ops:
  0.6 0.0 copy-start
  1.3 23.5 %exchange.1 = (bf16[32,4096]{1,0:T(8,128)(2,1)S(1)}, f32[8,128]{1,0:T(8,128)S(1)}, f32[2,32,128]{2,1,0:T(8,128)S(1)}, bf16[512,4096]{1,0:T(8,128)(2,1)S(1)}) custom-call(s32[16]{0:T(128)} %bins_ref.1, f32[64,2,4096]{2,1,0:T(2,128)} %snap_ref.1, bf16[4,2,32,2,4096]{4,3,2,1,0:T(2,128)(2,1)} %basis_ref.1), custom_call_target="tpu_custom_call" | custom-call | tf_op jit(solution)/shard_map/exchange/pallas_call | solution.py:284
  24.8 0.0 copy-done
  24.8 4.3 %update.1 = (bf16[4,2,32,2,4096]{4,3,2,1,0:T(2,128)(2,1)}, f32[4,2,32,32]{3,2,1,0:T(8,128)}) custom-call(s32[1]{0:T(128)S(6)} %copy.7.count_ref, f32[4,32]{1,0:T(4,128)S(1)} %copy-done, f32[8,128]{1,0:T(8,128)S(1)} %get-tuple-element.6.coef_ref, f32[2,32,128]{2,1,0:T(8,128)S(1)} %get-tuple-element.7.gram_ref, ...), custom_call_target="tpu_custom_call" | custom-call | tf_op jit(solution)/shard_map/update/pallas_call | solution.py:314
Async XLA Ops:
  0.6 24.2 %copy-start = (f32[4,32]{1,0:T(4,128)S(1)}, f32[4,32]{1,0:T(4,128)}, u32[]{:S(2)}) copy-start(f32[4,32]{1,0:T(4,128)} %eig_ref.1) | copy-start | bytes 1540
